TPU v7x, 32 devices: a whole 2x2x4 slice. The times are simulated.
32 devices in a mesh: grp: 2 (over x), dev: 16 (over z, y, core).
Axes of the slice: x: 2, y: 2, z: 4, core: 2. Of those that a mesh axis runs over, the one named last changes fastest.
Arguments:
- stream: bfloat16 [512, 4096], P('grp'), may hold values from -6 to 6
- row_length: int32 [4], P('grp'), may hold values from 1 to 128, as said below
- row_start: int32 [4], P('grp'), may hold values from 0 to 2047
- attn_gain: float32 [4096], replicated, may hold values from 0.1 to 1.9
- w_query: bfloat16 [4096, 4096], P('grp', 'dev'), as said below
- w_key: bfloat16 [4096, 1024], P('grp', 'dev'), may hold values from -0.09375 to 0.09375
- w_value: bfloat16 [4096, 1024], P('grp', 'dev'), may hold values from -0.09375 to 0.09375
- w_out: bfloat16 [4096, 4096], P('grp', 'dev'), may hold values from -0.09375 to 0.09375
- ffn_gain: float32 [4096], replicated, may hold values from 0.1 to 1.9
- w_gate: bfloat16 [4096, 14336], P('grp', 'dev'), may hold values from -0.09375 to 0.09375
- w_up: bfloat16 [4096, 14336], P('grp', 'dev'), may hold values from -0.09375 to 0.09375
- w_down: bfloat16 [4096, 14336], P('grp', 'dev'), may hold values from -0.046875 to 0.046875
Outputs:
- key_cache: bfloat16 [512, 1024], P('grp', 'dev')
- value_cache: bfloat16 [512, 1024], P('grp', 'dev')
- next_stream: bfloat16 [512, 4096], P('grp', 'dev')
Inputs may be any that keep to these rules, and one draw needn't show every extreme that they name: `row_length`: in every draw some row holds all 128 slots cached and some row only one. `row_start`: position of each row's first slot. `w_query`: query projection with independent entries.
All inputs are finite; a program needn't handle non-finite values.
Results may differ from a plain program's by a relative error of at most 0.011.
The roundings to bfloat16 on the way count: a program that leaves them out, or rounds other values in their place, can miss the bound.
Values may be sent and summed in bfloat16 or wider, within the bound.
A program may use at most 128 MiB of HBM per device.

v0:
```python
import math

import jax
import jax.numpy as jnp
from jax import lax
from jax.sharding import PartitionSpec as P

HEADS = 32
KV_HEADS = 8
HEAD_DIM = 128
ROW_LEN = 128


rope_base = 500000.0


def norm_rows(values, gain):
    return values * lax.rsqrt(jnp.mean(values * values, axis=-1, keepdims=True) + 1e-05) * gain


def rotate(values, positions, first):
    cols = first + jnp.arange(values.shape[1], dtype=jnp.int32)
    pair = (cols % HEAD_DIM // 2).astype(jnp.float32)
    freq = jnp.exp(-(2.0 * pair / HEAD_DIM) * math.log(rope_base))
    angle = positions.astype(jnp.float32)[:, None] * freq[None, :]
    lead = values.reshape(values.shape[0], -1, 2)
    partner = jnp.stack([-lead[..., 1], lead[..., 0]], axis=-1).reshape(values.shape)
    return values * jnp.cos(angle) + partner * jnp.sin(angle)


def attend(queries, keys, values, offset, length):
    group = HEADS // KV_HEADS
    count = queries.shape[0]
    qh = queries.reshape(count, KV_HEADS, group, HEAD_DIM)
    kh = keys.reshape(-1, KV_HEADS, HEAD_DIM)
    vh = values.reshape(-1, KV_HEADS, HEAD_DIM)
    scores = jnp.einsum("qkgd,jkd->kgqj", qh, kh, preferred_element_type=jnp.float32) / math.sqrt(
        HEAD_DIM
    )
    query_pos = offset + jnp.arange(count, dtype=jnp.int32)
    key_pos = jnp.arange(keys.shape[0], dtype=jnp.int32)
    allowed = (key_pos[None, :] <= query_pos[:, None]) & (key_pos[None, :] < length)
    scores = jnp.where(allowed, scores, -jnp.inf)
    top = jnp.max(scores, axis=-1, keepdims=True)
    expo = jnp.exp(scores - top)
    probs = (expo / jnp.sum(expo, axis=-1, keepdims=True)).astype(jnp.bfloat16)
    mixed = jnp.einsum("kgqj,jkd->qkgd", probs, vh, preferred_element_type=jnp.float32)
    return mixed.astype(jnp.bfloat16).reshape(count, -1)


def on_device(
    stream,
    row_length,
    row_start,
    attn_gain,
    w_query,
    w_key,
    w_value,
    w_out,
    ffn_gain,
    w_gate,
    w_up,
    w_down,
):
    member = lax.axis_index("dev")
    members = lax.axis_size("dev")
    w_query, w_key, w_value, w_out, w_gate, w_up, w_down = (
        lax.all_gather(w_query, "grp", axis=0, tiled=True),
        lax.all_gather(w_key, "grp", axis=0, tiled=True),
        lax.all_gather(w_value, "grp", axis=0, tiled=True),
        lax.all_gather(w_out, "grp", axis=0, tiled=True),
        lax.all_gather(w_gate, "grp", axis=0, tiled=True),
        lax.all_gather(w_up, "grp", axis=0, tiled=True),
        lax.all_gather(w_down, "grp", axis=0, tiled=True),
    )
    slots = stream.shape[0]
    query_cols = w_query.shape[1]
    kv_cols = w_key.shape[1]
    positions = (row_start[:, None] + jnp.arange(ROW_LEN, dtype=jnp.int32)[None, :]).reshape(-1)
    normed = norm_rows(stream.astype(jnp.float32), attn_gain).astype(jnp.bfloat16)
    queries = rotate(
        jnp.dot(normed, w_query, preferred_element_type=jnp.float32), positions, member * query_cols
    ).astype(jnp.bfloat16)
    keys = rotate(
        jnp.dot(normed, w_key, preferred_element_type=jnp.float32), positions, member * kv_cols
    ).astype(jnp.bfloat16)
    values = jnp.dot(normed, w_value, preferred_element_type=jnp.float32).astype(jnp.bfloat16)
    share = slots // members
    first = member * share
    all_queries, all_keys, all_values = (
        lax.all_gather(queries, "dev", axis=1, tiled=True),
        lax.all_gather(keys, "dev", axis=1, tiled=True),
        lax.all_gather(values, "dev", axis=1, tiled=True),
    )
    own_queries = lax.dynamic_slice_in_dim(all_queries, first, share, 0)
    row_index = first // ROW_LEN
    row_keys = lax.dynamic_slice_in_dim(all_keys, row_index * ROW_LEN, ROW_LEN, 0)
    row_values = lax.dynamic_slice_in_dim(all_values, row_index * ROW_LEN, ROW_LEN, 0)
    length = lax.dynamic_index_in_dim(row_length, row_index, 0, keepdims=False)
    mixed = attend(own_queries, row_keys, row_values, first - row_index * ROW_LEN, length)
    projected = jnp.dot(
        lax.all_gather(mixed, "dev", axis=0, tiled=True), w_out, preferred_element_type=jnp.float32
    )
    own_stream = lax.dynamic_slice_in_dim(stream, member * query_cols, query_cols, 1)
    attended = (own_stream.astype(jnp.float32) + projected).astype(jnp.bfloat16)
    full_rows = lax.all_gather(attended, "dev", axis=1, tiled=True)
    normed2 = norm_rows(full_rows.astype(jnp.float32), ffn_gain).astype(jnp.bfloat16)
    gate = jnp.dot(normed2, w_gate, preferred_element_type=jnp.float32)
    up = jnp.dot(normed2, w_up, preferred_element_type=jnp.float32)
    hidden = (jax.nn.silu(gate) * up).astype(jnp.bfloat16)
    partial_down = lax.dot_general(
        hidden, w_down, (((1,), (1,)), ((), ())), preferred_element_type=jnp.float32
    )
    summed = lax.psum_scatter(partial_down, "dev", scatter_dimension=1, tiled=True)
    next_stream = (attended.astype(jnp.float32) + summed).astype(jnp.bfloat16)
    return (keys, values, next_stream)


def solution(mesh):
    placed = (
        P("grp", None),
        P("grp"),
        P("grp"),
        P(),
        P("grp", "dev"),
        P("grp", "dev"),
        P("grp", "dev"),
        P("grp", "dev"),
        P(),
        P("grp", "dev"),
        P("grp", "dev"),
        P("grp", "dev"),
    )
    return jax.shard_map(
        on_device,
        mesh=mesh,
        in_specs=placed,
        out_specs=(P("grp", "dev"), P("grp", "dev"), P("grp", "dev")),
        check_vma=False,
    )
```

profile of v0, /device:TPU:10, one launch (start us, length us, event | category | flops | bytes accessed | tf_op | source)
XLA Modules:
  0.0 585.3 jit_solution(3967756529410625738)
XLA Ops:
  8.7 2.1 fusion.1
  10.8 32.1 %all-gather.9.cloned.1.call-done = bf16[4096,256]{1,0:T(8,128)(2,1)} async-done(((bf16[2048,256]{1,0:T(8,128)(2,1)}), bf16[4096,256]{1,0:T(8,128)(2,1)}) %all-gather.9.cloned.1.call-update) | async-done | bytes 2097168 | tf_op jit(solution)/shard_map/all_gather | solution.py:68
  42.9 3.4 fusion.34
  47.1 1.8 fusion.22
  49.7 8.7 %all_gather.36 = bf16[4096,64]{0,1:T(8,128)(2,1)S(1)} all-gather(bf16[2048,64]{0,1:T(8,128)(2,1)S(1)} %copy-done.3), channel_id=1, replica_groups=mesh['grp'=2,'dev'=16] {'grp'}, dimensions={0}, use_global_device_ids=true | all-gather | bytes 786432 | tf_op jit(solution)/shard_map/all_gather | solution.py:69
  58.5 0.8 fusion.37
  59.9 20.8 %all_gather.39 = bf16[256,1024]{0,1:T(8,128)(2,1)S(1)} all-gather(bf16[256,64]{0,1:T(8,128)(2,1)S(1)} %fusion.27), channel_id=1, replica_groups=mesh['grp'=2,'dev'=16] {'dev'}, dimensions={1}, use_global_device_ids=true | all-gather | bytes 557056 | tf_op jit(solution)/shard_map/all_gather | solution.py:92
  82.0 9.3 %all_gather.37 = bf16[4096,64]{0,1:T(8,128)(2,1)S(1)} all-gather(bf16[2048,64]{0,1:T(8,128)(2,1)S(1)} %copy-done.4), channel_id=1, replica_groups=mesh['grp'=2,'dev'=16] {'grp'}, dimensions={0}, use_global_device_ids=true | all-gather | bytes 786432 | tf_op jit(solution)/shard_map/all_gather | solution.py:70
  91.2 0.8 convolution_convert_fusion.1
  92.1 19.0 %all_gather.38 = bf16[256,1024]{0,1:T(8,128)(2,1)S(1)} all-gather(bf16[256,64]{0,1:T(8,128)(2,1)S(1)} %convolution_convert_fusion.1), channel_id=1, replica_groups=mesh['grp'=2,'dev'=16] {'dev'}, dimensions={1}, use_global_device_ids=true | all-gather | bytes 557056 | tf_op jit(solution)/shard_map/all_gather | solution.py:93
  111.2 1.6 constant_dynamic-slice_fusion
  113.4 0.9 fusion.13
  115.2 9.6 %all-gather.15.cloned.1.call-done = bf16[4096,256]{1,0:T(8,128)(2,1)} async-done(((bf16[2048,256]{1,0:T(8,128)(2,1)}), bf16[4096,256]{1,0:T(8,128)(2,1)}) %all-gather.15.cloned.1.call-update) | async-done | bytes 2097168 | tf_op jit(solution)/shard_map/all_gather | solution.py:71
  124.8 44.0 %all-gather.13.cloned.1.call-done = bf16[256,4096]{1,0:T(8,128)(2,1)} async-done(((bf16[16,4096]{1,0:T(8,128)(2,1)}), bf16[256,4096]{1,0:T(8,128)(2,1)}) %all-gather.13.cloned.1.call-update) | async-done | bytes 2097168 | tf_op jit(solution)/shard_map/all_gather | solution.py:102
  168.7 3.6 fusion.12
  174.7 38.3 %all-gather.17.cloned.1.call-done = bf16[256,4096]{1,0:T(8,128)(2,1)} async-done(((bf16[256,256]{1,0:T(8,128)(2,1)}), bf16[256,4096]{1,0:T(8,128)(2,1)}) %all-gather.17.cloned.1.call-update) | async-done | bytes 2097168 | tf_op jit(solution)/shard_map/all_gather | solution.py:106
  213.0 2.1 fusion.4
  215.1 90.0 %all-gather.19.cloned.1.call-done = bf16[4096,896]{1,0:T(8,128)(2,1)} async-done(((bf16[2048,896]{1,0:T(8,128)(2,1)}), bf16[4096,896]{1,0:T(8,128)(2,1)}) %all-gather.19.cloned.1.call-update) | async-done | bytes 7340048 | tf_op jit(solution)/shard_map/all_gather | solution.py:72
  305.1 6.1 %fusion.17 = f32[256,896]{1,0:T(8,128)S(1)} fusion(bf16[4096,896]{1,0:T(8,128)(2,1)} %all-gather.19.cloned.1.call-done, bf16[256,4096]{1,0:T(8,128)(2,1)} %all-gather.17.cloned.1.call-done, f32[4096]{0:T(1024)S(1)} %copy-done.8, f32[256]{0:T(256)S(1)} %add_rsqrt_fusion), kind=kOutput, calls=%fused_computation.24 | convolution fusion | flops 1883242496 | bytes 10372096 | tf_op jit(solution)/shard_map/dot_general | solution.py:108
  311.2 87.6 %all-gather.21.cloned.1.call-done = bf16[4096,896]{1,0:T(8,128)(2,1)} async-done(((bf16[2048,896]{1,0:T(8,128)(2,1)}), bf16[4096,896]{1,0:T(8,128)(2,1)}) %all-gather.21.cloned.1.call-update) | async-done | bytes 7340048 | tf_op jit(solution)/shard_map/all_gather | solution.py:73
  398.8 93.8 %all-gather.23.cloned.1.call-done = bf16[4096,896]{1,0:T(8,128)(2,1)} async-done(((bf16[2048,896]{1,0:T(8,128)(2,1)}), bf16[4096,896]{1,0:T(8,128)(2,1)}) %all-gather.23.cloned.1.call-update) | async-done | bytes 7340048 | tf_op jit(solution)/shard_map/all_gather | solution.py:74
  492.6 11.8 %fusion.14 = f32[256,4096]{1,0:T(8,128)} fusion(bf16[4096,896]{1,0:T(8,128)(2,1)} %all-gather.23.cloned.1.call-done, bf16[4096,896]{1,0:T(8,128)(2,1)} %all-gather.21.cloned.1.call-done, f32[256,896]{1,0:T(8,128)S(1)} %fusion.17, bf16[256,4096]{1,0:T(8,128)(2,1)S(1)} %copy-done.1, f32[4096]{0:T(1024)S(1)} %copy-done.8, f32[256]{0:T(256)S(1)} %add_rsqrt_fusion), kind=kOutput, calls=%fused_computation.23 | convolution fusion | flops 3763666944 | bytes 21906432 | tf_op jit(solution)/shard_map/dot_general | solution.py:111
  504.4 72.7 %reduce-scatter.2.cloned.1.call-done = f32[256,256]{1,0:T(8,128)} async-done(((f32[256,4096]{1,0:T(8,128)}), f32[256,256]{1,0:T(8,128)}) %reduce-scatter.2.cloned.1.call-update) | async-done | bytes 262160 | tf_op jit(solution)/shard_map/reduce_scatter | solution.py:114
  577.1 1.6 add_convert_fusion
  (63 shorter events, 8.8 us)
Async XLA Ops:
  7.2 35.8 %all-gather.9.cloned.1.call-start = ((), (), s32[]{:S(2)}) async-start(), calls=%async_computation.1 | async-start | bytes 3145728 | tf_op jit(solution)/shard_map/all_gather | solution.py:68
  7.9 103.3 %all-gather.11.cloned.1.call-start = ((), (), s32[]{:S(2)}) async-start(), calls=%async_computation.2 | async-start | bytes 2228224 | tf_op jit(solution)/shard_map/all_gather | solution.py:91
  10.8 38.9 %copy-start.3 = (bf16[2048,64]{0,1:T(8,128)(2,1)S(1)}, bf16[2048,64]{0,1:T(8,128)(2,1)}, u32[]{:S(2)}) copy-start(bf16[2048,64]{0,1:T(8,128)(2,1)} %param.17) | copy-start | bytes 786436
  10.8 47.7 %copy-start = (bf16[256,4096]{1,0:T(8,128)(2,1)S(1)}, bf16[256,4096]{1,0:T(8,128)(2,1)}, u32[]{:S(2)}) copy-start(bf16[256,4096]{1,0:T(8,128)(2,1)} %param.12) | copy-start | bytes 6291460
  10.8 47.6 %copy-start.7 = (f32[4096]{0:T(1024)S(1)}, f32[4096]{0:T(1024)}, u32[]{:S(2)}) copy-start(f32[4096]{0:T(1024)} %param.15) | copy-start | bytes 49156
  47.1 33.6 %copy-start.9 = (s32[2]{0:T(128)S(1)}, s32[2]{0:T(128)}, u32[]{:S(2)}) copy-start(s32[2]{0:T(128)} %param.13) | copy-start | bytes 28
  47.1 34.8 %copy-start.4 = (bf16[2048,64]{0,1:T(8,128)(2,1)S(1)}, bf16[2048,64]{0,1:T(8,128)(2,1)}, u32[]{:S(2)}) copy-start(bf16[2048,64]{0,1:T(8,128)(2,1)} %param.18) | copy-start | bytes 786436
  48.9 75.8 %all-gather.15.cloned.1.call-start = ((), (), s32[]{:S(2)}) async-start(), calls=%async_computation.4 | async-start | bytes 3145728 | tf_op jit(solution)/shard_map/all_gather | solution.py:71
  49.7 119.1 %all-gather.13.cloned.1.call-start = ((), (), s32[]{:S(2)}) async-start(), calls=%async_computation.3 | async-start | bytes 2228224 | tf_op jit(solution)/shard_map/all_gather | solution.py:102
  59.9 52.9 %copy-start.5 = (bf16[256,64]{0,1:T(8,128)(2,1)}, bf16[256,64]{0,1:T(8,128)(2,1)S(1)}, u32[]{:S(2)}) copy-start(bf16[256,64]{0,1:T(8,128)(2,1)S(1)} %fusion.27) | copy-start | bytes 98308
  92.1 80.3 %copy-start.6 = (bf16[256,64]{0,1:T(8,128)(2,1)}, bf16[256,64]{0,1:T(8,128)(2,1)S(1)}, u32[]{:S(2)}) copy-start(bf16[256,64]{0,1:T(8,128)(2,1)S(1)} %convolution_convert_fusion.1) | copy-start | bytes 98308
  115.2 97.8 %all-gather.17.cloned.1.call-start = ((), (), s32[]{:S(2)}) async-start(), calls=%async_computation.5 | async-start | bytes 2228224 | tf_op jit(solution)/shard_map/all_gather | solution.py:106
  172.4 132.7 %all-gather.19.cloned.1.call-start = ((), (), s32[]{:S(2)}) async-start(), calls=%async_computation.6 | async-start | bytes 11010048 | tf_op jit(solution)/shard_map/all_gather | solution.py:72
  172.9 132.1 %copy-start.8 = (f32[4096]{0:T(1024)S(1)}, f32[4096]{0:T(1024)}, u32[]{:S(2)}) copy-start(f32[4096]{0:T(1024)} %param.20) | copy-start | bytes 49156
  173.0 225.9 %all-gather.21.cloned.1.call-start = ((), (), s32[]{:S(2)}) async-start(), calls=%async_computation.7 | async-start | bytes 11010048 | tf_op jit(solution)/shard_map/all_gather | solution.py:73
  173.7 318.9 %all-gather.23.cloned.1.call-start = ((), (), s32[]{:S(2)}) async-start(), calls=%async_computation.8 | async-start | bytes 11010048 | tf_op jit(solution)/shard_map/all_gather | solution.py:74
  174.5 402.7 %reduce-scatter.2.cloned.1.call-start = ((), (), s32[]{:S(2)}) async-start(), calls=%async_computation.9 | async-start | bytes 4456448 | tf_op jit(solution)/shard_map/reduce_scatter | solution.py:114
  215.1 277.6 %copy-start.1 = (bf16[256,4096]{1,0:T(8,128)(2,1)S(1)}, bf16[256,4096]{1,0:T(8,128)(2,1)}, u32[]{:S(2)}) copy-start(bf16[256,4096]{1,0:T(8,128)(2,1)} %all-gather.17.cloned.1.call-done) | copy-start | bytes 6291460
  504.4 72.8 %copy-start.2 = (bf16[256,256]{1,0:T(8,128)(2,1)S(1)}, bf16[256,256]{1,0:T(8,128)(2,1)}, u32[]{:S(2)}) copy-start(bf16[256,256]{1,0:T(8,128)(2,1)} %fusion.12) | copy-start | bytes 393220
Sparse Core Ops, SparseCore 0:
  9.5 33.3 all-gather.8
  49.0 42.1 all-gather.10
  92.8 31.9 all-gather.14
  127.4 41.3 all-gather.12
  172.5 40.4 all-gather.16
  214.4 90.6 all-gather.18
  306.6 92.1 all-gather.20
  400.4 92.1 all-gather.22
  504.5 72.5 reduce-scatter.1
where the time goes:
time: 588 us; the launch traced here: 585 us
  waiting for transfers between devices  471 us (80%)
  blocking collectives  57.8 us (10%)
  matrix products  27.8 us (5%)
  between operations  14.1 us (2%)
  other arithmetic  10.2 us (2%)
    all_gather x1, waiting for transfers between devices, on_device(): lax.all_gather(w_down, 'grp', axis=0, tiled=True)  93.8 us
    all_gather x1, waiting for transfers between devices, on_device(): lax.all_gather(w_gate, 'grp', axis=0, tiled=True)  90 us
    all_gather x1, waiting for transfers between devices, on_device(): lax.all_gather(w_up, 'grp', axis=0, tiled=True)  87.6 us
    reduce_scatter x1, waiting for transfers between devices, on_device(): lax.psum_scatter(partial_down, 'dev', scatter_dimension=1, tiled=True)  72.7 us
    all_gather x1, waiting for transfers between devices, on_device(): lax.all_gather(mixed, 'dev', axis=0, tiled=True)  44 us
    all_gather x1, waiting for transfers between devices, on_device(): full_rows = lax.all_gather(attended, 'dev', axis=1, tiled=True)  38.3 us
    all_gather x1, waiting for transfers between devices, on_device(): lax.all_gather(w_query, 'grp', axis=0, tiled=True)  32.1 us
    all_gather x1, blocking collectives, on_device(): lax.all_gather(keys, 'dev', axis=1, tiled=True)  20.8 us
  transfers between devices with their start and end apart: 9, of which 8 were waited for; matrix products, arithmetic and copies ran while one was open for 3% of the time, Pallas kernels for 0%

commit v1 on v0

--- a/solution.py
+++ b/solution.py
@@ -48,7 +48,7 @@
     return mixed.astype(jnp.bfloat16).reshape(count, -1)
 
 
-def on_device(
+def gathered_weights(
     stream,
     row_length,
     row_start,
@@ -116,7 +116,220 @@
     return (keys, values, next_stream)
 
 
+def across(values):
+    return lax.ppermute(values, "grp", [(0, 1), (1, 0)])
+
+
+def beside(values, bit):
+    members = lax.axis_size("dev")
+    return lax.ppermute(values, "dev", [(i, i ^ bit) for i in range(members)])
+
+
+def corner(values):
+    members = lax.axis_size("dev")
+    top = members // 2
+    pairs = []
+    for grp in range(2):
+        for dev in range(members):
+            if dev // top != grp:
+                pairs.append((grp * members + dev, (1 - grp) * members + (dev ^ top)))
+    return lax.ppermute(values, ("grp", "dev"), pairs)
+
+
+def pick(values, index, axis):
+    return lax.dynamic_index_in_dim(values, index, axis, keepdims=False)
+
+
+def after(values, *earlier):
+    return lax.optimization_barrier((values,) + earlier)[0]
+
+
+def turn(values, cos, sin):
+    even = jnp.arange(values.shape[1], dtype=jnp.int32) % 2 == 0
+    partner = jnp.where(even[None, :], -jnp.roll(values, -1, axis=1), jnp.roll(values, 1, axis=1))
+    return values * cos + partner * sin
+
+
+def halve(values, axis, bit, mine):
+    return pick(values, mine, axis) + beside(pick(values, 1 - mine, axis), bit)
+
+
+def dot(a, b):
+    return jnp.dot(a, b, preferred_element_type=jnp.float32)
+
+
+def dot_t(a, b):
+    return lax.dot_general(a, b, (((1,), (1,)), ((), ())), preferred_element_type=jnp.float32)
+
+
+def moved_rows(
+    stream,
+    row_length,
+    row_start,
+    attn_gain,
+    w_query,
+    w_key,
+    w_value,
+    w_out,
+    ffn_gain,
+    w_gate,
+    w_up,
+    w_down,
+):
+    grp = lax.axis_index("grp")
+    member = lax.axis_index("dev")
+    members = lax.axis_size("dev")
+    core, y, z_lo = member % 2, member // 2 % 2, member // 4 % 2
+    slots, width = stream.shape
+    half = width // 2
+    part = slots // 2
+    block = w_query.shape[1]
+    kv_cols = w_key.shape[1]
+    rows = slots // ROW_LEN
+    blocks = half // block
+
+    normed = norm_rows(stream.astype(jnp.float32), attn_gain).astype(jnp.bfloat16)
+    got = across(lax.dynamic_slice(normed, (core * part, (1 - grp) * half), (part, half)))
+    sib = beside(got, 1)
+    w_all = jnp.concatenate([w_query, w_key, w_value], axis=1)
+    back_got = across(dot(got, w_all))
+    back_sib = across(dot(sib, w_all))
+    own = dot(lax.dynamic_slice_in_dim(normed, grp * half, half, 1), w_all)
+    lo = jnp.where(core == 0, back_got, back_sib)
+    hi = jnp.where(core == 0, back_sib, back_got)
+    total = own + jnp.concatenate([lo, hi], axis=0)
+
+    positions = (row_start[:, None] + jnp.arange(ROW_LEN, dtype=jnp.int32)[None, :]).reshape(-1)
+    pair = (jnp.arange(HEAD_DIM, dtype=jnp.int32) // 2).astype(jnp.float32)
+    freq = jnp.exp(-(2.0 * pair / HEAD_DIM) * math.log(rope_base))
+    angle = positions.astype(jnp.float32)[:, None] * freq[None, :]
+    cos, sin = jnp.cos(angle), jnp.sin(angle)
+    heads = block // HEAD_DIM
+    queries = turn(
+        total[:, :block], jnp.tile(cos, (1, heads)), jnp.tile(sin, (1, heads))
+    ).astype(jnp.bfloat16)
+    key_first = core * kv_cols
+    keys = turn(
+        total[:, block : block + kv_cols],
+        lax.dynamic_slice_in_dim(cos, key_first, kv_cols, 1),
+        lax.dynamic_slice_in_dim(sin, key_first, kv_cols, 1),
+    ).astype(jnp.bfloat16)
+    values = total[:, block + kv_cols :].astype(jnp.bfloat16)
+
+    mine = jnp.stack([keys, values])
+    theirs = beside(mine, 1)
+    both = jnp.where(
+        core == 0,
+        jnp.concatenate([mine, theirs], axis=2),
+        jnp.concatenate([theirs, mine], axis=2),
+    )
+    qh = queries.reshape(rows, ROW_LEN, heads, HEAD_DIM)
+    kh = both[0].reshape(rows, ROW_LEN, HEAD_DIM)
+    vh = both[1].reshape(rows, ROW_LEN, HEAD_DIM)
+    scores = jnp.einsum("rqhd,rjd->rhqj", qh, kh, preferred_element_type=jnp.float32) / math.sqrt(
+        HEAD_DIM
+    )
+    at = jnp.arange(ROW_LEN, dtype=jnp.int32)
+    allowed = (at[None, None, :] <= at[None, :, None]) & (
+        at[None, None, :] < row_length[:, None, None]
+    )
+    scores = jnp.where(allowed[:, None], scores, -jnp.inf)
+    top = jnp.max(scores, axis=-1, keepdims=True)
+    expo = jnp.exp(scores - top)
+    probs = (expo / jnp.sum(expo, axis=-1, keepdims=True)).astype(jnp.bfloat16)
+    mixed = jnp.einsum("rhqj,rjd->rqhd", probs, vh, preferred_element_type=jnp.float32)
+    mixed = mixed.astype(jnp.bfloat16).reshape(slots, block)
+
+    w_out_far = across(after(w_out, back_got, back_sib))
+    all_mixed = lax.all_gather(mixed, "dev", axis=0, tiled=False)
+
+    def by_blocks(blocked, weight):
+        return lax.dot_general(
+            blocked,
+            weight.reshape(blocks, block, -1),
+            (((0, 2), (0, 1)), ((), ())),
+            preferred_element_type=jnp.float32,
+        )
+
+    projected = by_blocks(
+        lax.dynamic_slice_in_dim(all_mixed, grp * blocks, blocks, 0), w_out
+    ) + by_blocks(lax.dynamic_slice_in_dim(all_mixed, (1 - grp) * blocks, blocks, 0), w_out_far)
+    own_stream = lax.dynamic_slice_in_dim(stream, member * block, block, 1)
+    attended = (own_stream.astype(jnp.float32) + projected).astype(jnp.bfloat16)
+    all_attended = lax.all_gather(attended, "dev", axis=0, tiled=False)
+    far_attended = corner(attended)
+
+    wide = all_attended.astype(jnp.float32)
+    mean = jnp.mean(jnp.mean(wide * wide, axis=2, keepdims=True), axis=0, keepdims=True)
+    normed2 = (
+        wide * lax.rsqrt(mean + 1e-05) * ffn_gain.reshape(members, 1, block)
+    ).astype(jnp.bfloat16)
+    got2 = across(
+        lax.dynamic_slice(normed2, ((1 - grp) * blocks, core * part, 0), (blocks, part, block))
+    )
+    sib2 = beside(got2, 1)
+    gate_got = across(by_blocks(got2, w_gate))
+    up_got = across(by_blocks(got2, w_up))
+    gate_sib = across(by_blocks(sib2, w_gate))
+    up_sib = across(by_blocks(sib2, w_up))
+    near = lax.dynamic_slice_in_dim(normed2, grp * blocks, blocks, 0)
+    near_got = lax.dynamic_slice_in_dim(near, core * part, part, 1)
+    near_sib = lax.dynamic_slice_in_dim(near, (1 - core) * part, part, 1)
+
+    def gated(rows_near, gate_far, up_far):
+        gate = by_blocks(rows_near, w_gate) + gate_far
+        up = by_blocks(rows_near, w_up) + up_far
+        return (jax.nn.silu(gate) * up).astype(jnp.bfloat16)
+
+    hidden_got = gated(near_got, gate_got, up_got)
+    hidden_sib = gated(near_sib, gate_sib, up_sib)
+    far_got = across(hidden_got)
+    far_sib = across(hidden_sib)
+
+    def placed(a, b):
+        lower = jnp.where(core == 0, a, b)
+        upper = jnp.where(core == 0, b, a)
+        return jnp.concatenate([lower, upper], axis=0)
+
+    near_hidden = placed(hidden_got, hidden_sib)
+    far_hidden = placed(far_got, far_sib)
+    w_pairs = w_down.reshape(blocks // 2, 2, block, -1)
+    w_send = pick(w_pairs, 1 - core, 1)
+    w_keep = pick(w_pairs, core, 1)
+
+    def down(rows_in, weight):
+        out = dot_t(rows_in, weight.reshape(-1, weight.shape[-1]))
+        return out.reshape(slots, blocks // 2, block)
+
+    def stage(rows_in):
+        return down(rows_in, w_keep) + beside(down(rows_in, w_send), 1)
+
+    near_sum, far_sum = stage(near_hidden), stage(far_hidden)
+
+    def folded(sums):
+        return jnp.moveaxis(sums, 1, 0).reshape(2, 2, slots, block)
+
+    is_near = member // (members // 2) == grp
+    near_sum, far_sum = folded(near_sum), folded(far_sum)
+    keep_all = jnp.stack([near_sum, far_sum])
+    side = jnp.where(is_near, 0, 1)
+    one, two = keep_all[:, :, :, :part], keep_all[:, :, :, part:]
+    one = halve(one, 2, 2, y)
+    two = halve(two, 1, 4, z_lo)
+    one = halve(one, 1, 4, z_lo)
+    two = halve(two, 0, 8, side)
+    one = halve(one, 0, 8, side)
+    two = halve(two, 0, 2, y)
+    summed = jnp.concatenate([one, two], axis=0)
+    base = jnp.where(is_near, attended, far_attended)
+    done = (base.astype(jnp.float32) + summed).astype(jnp.bfloat16)
+    next_stream = jnp.where(is_near, done, corner(done))
+    return (keys, values, next_stream)
+
+
 def solution(mesh):
+    exact = dict(mesh.shape) == {"grp": 2, "dev": 16}
+    on_device = moved_rows if exact else gathered_weights
     placed = (
         P("grp", None),
         P("grp"),

time: 588 us -> 271 us (0.46)
  waiting for transfers between devices: 471 us -> 185 us
  blocking collectives: 57.8 us -> 0 us
  starting transfers between devices: 0.53 us -> 26.8 us
    all_gather x8 -> x2, waiting for transfers between devices: 395 us -> 81.2 us  [the longest x1 40.9 us: moved_rows(): all_mixed = lax.all_gather(mixed, 'dev', axis=0, tiled=False)]
    ppermute x0 -> x24, waiting for transfers between devices: none -> 104 us  [the longest x11 73.7 us: across(): return lax.ppermute(values, 'grp', [(0, 1), (1, 0)])]
    reduce_scatter x1 -> x0, waiting for transfers between devices: 72.7 us -> none  [on_device(): lax.psum_scatter(partial_down, 'dev', scatter_dimension=1, tiled=True)]
    all_gather x4 -> x0, blocking collectives: 57.8 us -> none  [the longest x1 20.8 us: on_device(): lax.all_gather(keys, 'dev', axis=1, tiled=True)]
    ppermute x0 -> x24, starting transfers between devices: none -> 26.5 us  [the longest x11 11.4 us: beside(): return lax.ppermute(values, 'dev', [(i, i ^ bit) for i in range(members)])]
    dot_general x8 -> x19, matrix products: 27.8 us -> 21.7 us  [the longest x10 10.1 us: by_blocks(): lax.dot_general(blocked, weight.reshape(blocks, block, -1), (((0, 2), (0,...]
  transfers between devices with their start and end apart: 9 -> 26, of which waited for: 8 -> 19; matrix products, arithmetic and copies ran while one was open for 3% -> 9% of each run, Pallas kernels for 0% -> 0%
where the time goes in v1:
time: 271 us
  waiting for transfers between devices  185 us (68%)
  starting transfers between devices  26.8 us (10%)
  matrix products  22 us (8%)
  between operations  14.8 us (5%)
  other arithmetic  13.7 us (5%)
  local copies, waits for them, and re-layouts  8.33 us (3%)
    ppermute x11, waiting for transfers between devices, across(): return lax.ppermute(values, 'grp', [(0, 1), (1, 0)])  73.7 us
    all_gather x1, waiting for transfers between devices, moved_rows(): all_mixed = lax.all_gather(mixed, 'dev', axis=0, tiled=False)  40.9 us
    all_gather x1, waiting for transfers between devices, moved_rows(): all_attended = lax.all_gather(attended, 'dev', axis=0, tiled=False)  40.3 us
    ppermute x11, waiting for transfers between devices, beside(): return lax.ppermute(values, 'dev', [(i, i ^ bit) for i in range(members)])  25.3 us
    ppermute x11, starting transfers between devices, beside(): return lax.ppermute(values, 'dev', [(i, i ^ bit) for i in range(members)])  11.4 us
    ppermute x11, starting transfers between devices, across(): return lax.ppermute(values, 'grp', [(0, 1), (1, 0)])  10.3 us
    dot_general x10, matrix products, by_blocks(): lax.dot_general(blocked, weight.reshape(blocks, block, -1), (((0, 2), (0,...  10.1 us
    dot_general x4, matrix products, dot_t(): lax.dot_general(a, b, (((1,), (1,)), ((), ())), preferred_element_type=jn...  6.91 us
  transfers between devices with their start and end apart: 26, of which 19 were waited for; matrix products, arithmetic and copies ran while one was open for 9% of the time, Pallas kernels for 0%

profile of v1, /device:TPU:10, one launch (start us, length us, event | category | flops | bytes accessed | tf_op | source)
XLA Modules:
  0.0 270.8 jit_solution(1315843824399544979)
XLA Ops:
  7.2 2.2 fusion.1
  14.3 12.0 %collective-permute-done = bf16[128,2048]{1,0:T(8,128)(2,1)} collective-permute-done((bf16[128,2048]{1,0:T(8,128)(2,1)S(1)}, bf16[128,2048]{1,0:T(8,128)(2,1)}, u32[]{:S(2)}, u32[]{:S(2)}) %collective-permute-start) | collective-permute-done | bytes 524320 | tf_op jit(solution)/shard_map/ppermute | solution.py:120
  35.2 3.3 %collective-permute-done.1 = f32[128,384]{1,0:T(8,128)S(1)} collective-permute-done((f32[128,384]{1,0:T(8,128)S(1)}, f32[128,384]{1,0:T(8,128)S(1)}, u32[]{:S(2)}, u32[]{:S(2)}) %collective-permute-start.1) | collective-permute-done | bytes 196640 | tf_op jit(solution)/shard_map/ppermute | solution.py:120
  38.5 3.8 %collective-permute-done.3 = f32[128,384]{1,0:T(8,128)S(1)} collective-permute-done((f32[128,384]{1,0:T(8,128)S(1)}, f32[128,384]{1,0:T(8,128)S(1)}, u32[]{:S(2)}, u32[]{:S(2)}) %collective-permute-start.3) | collective-permute-done | bytes 196640 | tf_op jit(solution)/shard_map/ppermute | solution.py:120
  48.0 40.9 %all-gather.4.cloned.1.call-done = bf16[16,256,256]{2,1,0:T(8,128)(2,1)} async-done(((bf16[1,256,256]{2,1,0:T(8,128)(2,1)}), bf16[16,256,256]{2,1,0:T(8,128)(2,1)}) %all-gather.4.cloned.1.call-update) | async-done | bytes 2097168 | tf_op jit(solution)/shard_map/all_gather | solution.py:244
  90.9 2.3 fusion.31
  93.3 40.3 %all-gather.6.cloned.1.call-done = bf16[4096,256]{1,0:T(8,128)(2,1)} async-done(((bf16[256,256]{1,0:T(8,128)(2,1)}), bf16[4096,256]{1,0:T(8,128)(2,1)}) %all-gather.6.cloned.1.call-update) | async-done | bytes 2097168 | tf_op jit(solution)/shard_map/all_gather | solution.py:259
  133.6 2.4 fusion.4
  140.0 10.8 %collective-permute-done.7 = bf16[8,128,256]{2,1,0:T(8,128)(2,1)S(1)} collective-permute-done((bf16[8,128,256]{2,1,0:T(8,128)(2,1)S(1)}, bf16[8,128,256]{2,1,0:T(8,128)(2,1)S(1)}, u32[]{:S(2)}, u32[]{:S(2)}) %collective-permute-start.7) | collective-permute-done | bytes 524320 | tf_op jit(solution)/shard_map/ppermute | solution.py:120
  159.6 5.4 %collective-permute-done.8 = f32[128,896]{1,0:T(8,128)S(1)} collective-permute-done((f32[128,896]{1,0:T(8,128)S(1)}, f32[128,896]{1,0:T(8,128)S(1)}, u32[]{:S(2)}, u32[]{:S(2)}) %collective-permute-start.8) | collective-permute-done | bytes 458784 | tf_op jit(solution)/shard_map/ppermute | solution.py:120
  165.0 9.8 %collective-permute-done.9 = f32[128,896]{1,0:T(8,128)S(1)} collective-permute-done((f32[128,896]{1,0:T(8,128)S(1)}, f32[128,896]{1,0:T(8,128)S(1)}, u32[]{:S(2)}, u32[]{:S(2)}) %collective-permute-start.9) | collective-permute-done | bytes 458784 | tf_op jit(solution)/shard_map/ppermute | solution.py:120
  174.8 9.8 %collective-permute-done.11 = f32[128,896]{1,0:T(8,128)S(1)} collective-permute-done((f32[128,896]{1,0:T(8,128)S(1)}, f32[128,896]{1,0:T(8,128)S(1)}, u32[]{:S(2)}, u32[]{:S(2)}) %collective-permute-start.11) | collective-permute-done | bytes 458784 | tf_op jit(solution)/shard_map/ppermute | solution.py:120
  184.7 9.4 %collective-permute-done.12 = f32[128,896]{1,0:T(8,128)S(1)} collective-permute-done((f32[128,896]{1,0:T(8,128)S(1)}, f32[128,896]{1,0:T(8,128)S(1)}, u32[]{:S(2)}, u32[]{:S(2)}) %collective-permute-start.12) | collective-permute-done | bytes 458784 | tf_op jit(solution)/shard_map/ppermute | solution.py:120
  197.4 5.6 %collective-permute-done.14 = bf16[128,896]{1,0:T(8,128)(2,1)S(1)} collective-permute-done((bf16[128,896]{1,0:T(8,128)(2,1)S(1)}, bf16[128,896]{1,0:T(8,128)(2,1)S(1)}, u32[]{:S(2)}, u32[]{:S(2)}) %collective-permute-start.14) | collective-permute-done | bytes 229408 | tf_op jit(solution)/shard_map/ppermute | solution.py:120
  203.0 3.6 %collective-permute-done.15 = bf16[128,896]{1,0:T(8,128)(2,1)S(1)} collective-permute-done((bf16[128,896]{1,0:T(8,128)(2,1)S(1)}, bf16[128,896]{1,0:T(8,128)(2,1)S(1)}, u32[]{:S(2)}, u32[]{:S(2)}) %collective-permute-start.15) | collective-permute-done | bytes 229408 | tf_op jit(solution)/shard_map/ppermute | solution.py:120
  208.5 2.4 fusion.19
  217.5 2.6 collective-permute-start.6
  220.1 8.6 %collective-permute-done.17 = f32[2,2,128,256]{3,2,1,0:T(8,128)} collective-permute-done((f32[2,2,128,256]{3,2,1,0:T(8,128)}, f32[2,2,128,256]{3,2,1,0:T(8,128)}, u32[]{:S(2)}, u32[]{:S(2)}) %collective-permute-start.17) | collective-permute-done | bytes 524320 | tf_op jit(solution)/shard_map/ppermute | solution.py:125
  231.6 3.8 %collective-permute-start.21 = (f32[2,128,256]{2,1,0:T(8,128)S(1)}, f32[2,128,256]{2,1,0:T(8,128)S(1)}, u32[]{:S(2)}, u32[]{:S(2)}) collective-permute-start(f32[2,128,256]{2,1,0:T(8,128)S(1)} %dynamic-slice_bitcast_fusion.1), channel_id=1, source_target_pairs={{0,8},{1,9},{2,10},{3,11},{4,12},{5,13},{6,14},{7,15},{8,0},{9,1},... | collective-permute-start | bytes 786440 | tf_op jit(solution)/shard_map/ppermute | solution.py:125
  235.3 5.9 %collective-permute-done.18 = f32[2,128,256]{2,1,0:T(8,128)S(1)} collective-permute-done((f32[2,128,256]{2,1,0:T(8,128)S(1)}, f32[2,128,256]{2,1,0:T(8,128)S(1)}, u32[]{:S(2)}, u32[]{:S(2)}) %collective-permute-start.18) | collective-permute-done | bytes 262176 | tf_op jit(solution)/shard_map/ppermute | solution.py:125
  241.3 2.3 collective-permute-start.19
  243.6 5.8 %collective-permute-done.21 = f32[2,128,256]{2,1,0:T(8,128)S(1)} collective-permute-done((f32[2,128,256]{2,1,0:T(8,128)S(1)}, f32[2,128,256]{2,1,0:T(8,128)S(1)}, u32[]{:S(2)}, u32[]{:S(2)}) %collective-permute-start.21) | collective-permute-done | bytes 262176 | tf_op jit(solution)/shard_map/ppermute | solution.py:125
  251.0 3.5 %collective-permute-done.22 = f32[128,256]{1,0:T(8,128)S(1)} collective-permute-done((f32[128,256]{1,0:T(8,128)S(1)}, f32[128,256]{1,0:T(8,128)S(1)}, u32[]{:S(2)}, u32[]{:S(2)}) %collective-permute-start.22) | collective-permute-done | bytes 131104 | tf_op jit(solution)/shard_map/ppermute | solution.py:125
  258.2 5.1 %collective-permute-done.23 = bf16[256,256]{1,0:T(8,128)(2,1)S(1)} collective-permute-done((bf16[256,256]{1,0:T(8,128)(2,1)S(1)}, bf16[256,256]{1,0:T(8,128)(2,1)S(1)}, u32[]{:S(2)}, u32[]{:S(2)}) %collective-permute-start.23) | collective-permute-done | bytes 131104 | tf_op jit(solution)/shard_map/ppermute | solution.py:136
  (149 shorter events, 54.3 us)
Async XLA Ops:
  7.2 81.8 %all-gather.4.cloned.1.call-start = ((), (), s32[]{:S(2)}) async-start(), calls=%async_computation | async-start | bytes 2228224 | tf_op jit(solution)/shard_map/all_gather | solution.py:244
  12.4 13.8 %collective-permute-start = (bf16[128,2048]{1,0:T(8,128)(2,1)S(1)}, bf16[128,2048]{1,0:T(8,128)(2,1)}, u32[]{:S(2)}, u32[]{:S(2)}) collective-permute-start(bf16[128,2048]{1,0:T(8,128)(2,1)S(1)} %dynamic_slice.83), channel_id=1, source_target_pairs={{0,16},{16,0},{1,17},{17,1},{2,18},{18,2},{3,19},{19,3},{4,20},{20... | collective-permute-start | bytes 1572872 | tf_op jit(solution)/shard_map/ppermute | solution.py:120
  26.3 5.1 %collective-permute-start.2 = (bf16[128,2048]{1,0:T(8,128)(2,1)}, bf16[128,2048]{1,0:T(8,128)(2,1)}, u32[]{:S(2)}, u32[]{:S(2)}) collective-permute-start(bf16[128,2048]{1,0:T(8,128)(2,1)} %collective-permute-done), channel_id=1, source_target_pairs={{0,1},{1,0},{2,3},{3,2},{4,5},{5,4},{6,7},{7,6},{8,9},{9,8},{10,11... | collective-permute-start | bytes 1572872 | tf_op jit(solution)/shard_map/ppermute | solution.py:125
  30.8 7.8 %collective-permute-start.1 = (f32[128,384]{1,0:T(8,128)S(1)}, f32[128,384]{1,0:T(8,128)S(1)}, u32[]{:S(2)}, u32[]{:S(2)}) collective-permute-start(f32[128,384]{1,0:T(8,128)S(1)} %fusion.85), channel_id=1, source_target_pairs={{0,16},{16,0},{1,17},{17,1},{2,18},{18,2},{3,19},{19,3},{4,20},{20... | collective-permute-start | bytes 589832 | tf_op jit(solution)/shard_map/ppermute | solution.py:120
  33.0 9.4 %collective-permute-start.3 = (f32[128,384]{1,0:T(8,128)S(1)}, f32[128,384]{1,0:T(8,128)S(1)}, u32[]{:S(2)}, u32[]{:S(2)}) collective-permute-start(f32[128,384]{1,0:T(8,128)S(1)} %fusion.84), channel_id=1, source_target_pairs={{0,16},{16,0},{1,17},{17,1},{2,18},{18,2},{3,19},{19,3},{4,20},{20... | collective-permute-start | bytes 589832 | tf_op jit(solution)/shard_map/ppermute | solution.py:120
  47.2 86.4 %all-gather.6.cloned.1.call-start = ((), (), s32[]{:S(2)}) async-start(), calls=%async_computation.1 | async-start | bytes 2228224 | tf_op jit(solution)/shard_map/all_gather | solution.py:259
  47.4 43.5 %collective-permute-start.5 = (bf16[2048,256]{1,0:T(8,128)(2,1)}, bf16[2048,256]{1,0:T(8,128)(2,1)S(1)}, u32[]{:S(2)}, u32[]{:S(2)}) collective-permute-start(bf16[2048,256]{1,0:T(8,128)(2,1)} %param.19), channel_id=1, source_target_pairs={{0,16},{16,0},{1,17},{17,1},{2,18},{18,2},{3,19},{19,3},{4,20},{20... | collective-permute-start | bytes 3145736 | tf_op jit(solution)/shard_map/ppermute | solution.py:120
  136.7 14.2 %collective-permute-start.7 = (bf16[8,128,256]{2,1,0:T(8,128)(2,1)S(1)}, bf16[8,128,256]{2,1,0:T(8,128)(2,1)S(1)}, u32[]{:S(2)}, u32[]{:S(2)}) collective-permute-start(bf16[8,128,256]{2,1,0:T(8,128)(2,1)S(1)} %constant_dynamic-slice_fusion), channel_id=1, source_target_pairs={{0,16},{16,0},{1,17},{17,1},{2,18},{18,2},{3,19},{19,3},{4,20},{20... | collective-permute-start | bytes 1572872 | tf_op jit(solution)/shard_map/ppermute | solution.py:120
  150.9 3.6 %collective-permute-start.10 = (bf16[8,128,256]{2,1,0:T(8,128)(2,1)S(1)}, bf16[8,128,256]{2,1,0:T(8,128)(2,1)S(1)}, u32[]{:S(2)}, u32[]{:S(2)}) collective-permute-start(bf16[8,128,256]{2,1,0:T(8,128)(2,1)S(1)} %collective-permute-done.7), channel_id=1, source_target_pairs={{0,1},{1,0},{2,3},{3,2},{4,5},{5,4},{6,7},{7,6},{8,9},{9,8},{10,11... | collective-permute-start | bytes 1572872 | tf_op jit(solution)/shard_map/ppermute | solution.py:125
  151.6 13.4 %collective-permute-start.8 = (f32[128,896]{1,0:T(8,128)S(1)}, f32[128,896]{1,0:T(8,128)S(1)}, u32[]{:S(2)}, u32[]{:S(2)}) collective-permute-start(f32[128,896]{1,0:T(8,128)S(1)} %convolution_bitcast_fusion.6), channel_id=1, source_target_pairs={{0,16},{16,0},{1,17},{17,1},{2,18},{18,2},{3,19},{19,3},{4,20},{20... | collective-permute-start | bytes 1376264 | tf_op jit(solution)/shard_map/ppermute | solution.py:120
  153.0 21.9 %collective-permute-start.9 = (f32[128,896]{1,0:T(8,128)S(1)}, f32[128,896]{1,0:T(8,128)S(1)}, u32[]{:S(2)}, u32[]{:S(2)}) collective-permute-start(f32[128,896]{1,0:T(8,128)S(1)} %convolution_bitcast_fusion.4), channel_id=1, source_target_pairs={{0,16},{16,0},{1,17},{17,1},{2,18},{18,2},{3,19},{19,3},{4,20},{20... | collective-permute-start | bytes 1376264 | tf_op jit(solution)/shard_map/ppermute | solution.py:120
  155.2 29.4 %collective-permute-start.11 = (f32[128,896]{1,0:T(8,128)S(1)}, f32[128,896]{1,0:T(8,128)S(1)}, u32[]{:S(2)}, u32[]{:S(2)}) collective-permute-start(f32[128,896]{1,0:T(8,128)S(1)} %convolution_bitcast_fusion.2), channel_id=1, source_target_pairs={{0,16},{16,0},{1,17},{17,1},{2,18},{18,2},{3,19},{19,3},{4,20},{20... | collective-permute-start | bytes 1376264 | tf_op jit(solution)/shard_map/ppermute | solution.py:120
  156.6 37.5 %collective-permute-start.12 = (f32[128,896]{1,0:T(8,128)S(1)}, f32[128,896]{1,0:T(8,128)S(1)}, u32[]{:S(2)}, u32[]{:S(2)}) collective-permute-start(f32[128,896]{1,0:T(8,128)S(1)} %convolution_bitcast_fusion), channel_id=1, source_target_pairs={{0,16},{16,0},{1,17},{17,1},{2,18},{18,2},{3,19},{19,3},{4,20},{20... | collective-permute-start | bytes 1376264 | tf_op jit(solution)/shard_map/ppermute | solution.py:120
  194.4 8.6 %collective-permute-start.14 = (bf16[128,896]{1,0:T(8,128)(2,1)S(1)}, bf16[128,896]{1,0:T(8,128)(2,1)S(1)}, u32[]{:S(2)}, u32[]{:S(2)}) collective-permute-start(bf16[128,896]{1,0:T(8,128)(2,1)S(1)} %get-tuple-element.18), channel_id=1, source_target_pairs={{0,16},{16,0},{1,17},{17,1},{2,18},{18,2},{3,19},{19,3},{4,20},{20... | collective-permute-start | bytes 688136 | tf_op jit(solution)/shard_map/ppermute | solution.py:120
  195.1 11.6 %collective-permute-start.15 = (bf16[128,896]{1,0:T(8,128)(2,1)S(1)}, bf16[128,896]{1,0:T(8,128)(2,1)S(1)}, u32[]{:S(2)}, u32[]{:S(2)}) collective-permute-start(bf16[128,896]{1,0:T(8,128)(2,1)S(1)} %get-tuple-element.19), channel_id=1, source_target_pairs={{0,16},{16,0},{1,17},{17,1},{2,18},{18,2},{3,19},{19,3},{4,20},{20... | collective-permute-start | bytes 688136 | tf_op jit(solution)/shard_map/ppermute | solution.py:120
  197.3 11.1 %collective-permute-start.13 = (f32[256,4,256]{2,0,1:T(8,128)S(1)}, f32[256,4,256]{2,0,1:T(8,128)S(1)}, u32[]{:S(2)}, u32[]{:S(2)}) collective-permute-start(f32[256,4,256]{2,0,1:T(8,128)S(1)} %fusion.9), channel_id=1, source_target_pairs={{0,1},{1,0},{2,3},{3,2},{4,5},{5,4},{6,7},{7,6},{8,9},{9,8},{10,11... | collective-permute-start | bytes 3145736 | tf_op jit(solution)/shard_map/ppermute | solution.py:125
  214.4 14.3 %collective-permute-start.17 = (f32[2,2,128,256]{3,2,1,0:T(8,128)}, f32[2,2,128,256]{3,2,1,0:T(8,128)}, u32[]{:S(2)}, u32[]{:S(2)}) collective-permute-start(f32[2,2,128,256]{3,2,1,0:T(8,128)} %dynamic-slice_bitcast_fusion), channel_id=1, source_target_pairs={{0,2},{1,3},{2,0},{3,1},{4,6},{5,7},{6,4},{7,5},{8,10},{9,11},{10,... | collective-permute-start | bytes 1572872 | tf_op jit(solution)/shard_map/ppermute | solution.py:125
  215.9 15.6 %collective-permute-start.20 = (f32[2,2,128,256]{3,2,0,1:T(8,128)S(1)}, f32[2,2,128,256]{3,2,0,1:T(8,128)S(1)}, u32[]{:S(2)}, u32[]{:S(2)}) collective-permute-start(f32[2,2,128,256]{3,2,0,1:T(8,128)S(1)} %bitcast.177), channel_id=1, source_target_pairs={{0,4},{1,5},{2,6},{3,7},{4,0},{5,1},{6,2},{7,3},{8,12},{9,13},{10,... | collective-permute-start | bytes 1572872 | tf_op jit(solution)/shard_map/ppermute | solution.py:125
  217.5 37.0 %collective-permute-start.6 = (bf16[256,256]{1,0:T(8,128)(2,1)}, bf16[256,256]{1,0:T(8,128)(2,1)S(1)}, u32[]{:S(2)}, u32[]{:S(2)}) collective-permute-start(bf16[256,256]{1,0:T(8,128)(2,1)} %fusion.31), channel_id=1, source_target_pairs={{8,16},{9,17},{10,18},{11,19},{12,20},{13,21},{14,22},{15,23},{16,... | collective-permute-start | bytes 393224 | tf_op jit(solution)/shard_map/ppermute | solution.py:136
  229.9 11.4 %collective-permute-start.18 = (f32[2,128,256]{2,1,0:T(8,128)S(1)}, f32[2,128,256]{2,1,0:T(8,128)S(1)}, u32[]{:S(2)}, u32[]{:S(2)}) collective-permute-start(f32[2,128,256]{2,1,0:T(8,128)S(1)} %dynamic-slice_bitcast_fusion.2), channel_id=1, source_target_pairs={{0,4},{1,5},{2,6},{3,7},{4,0},{5,1},{6,2},{7,3},{8,12},{9,13},{10,... | collective-permute-start | bytes 786440 | tf_op jit(solution)/shard_map/ppermute | solution.py:125
  231.6 17.8 %collective-permute-start.21 = (f32[2,128,256]{2,1,0:T(8,128)S(1)}, f32[2,128,256]{2,1,0:T(8,128)S(1)}, u32[]{:S(2)}, u32[]{:S(2)}) collective-permute-start(f32[2,128,256]{2,1,0:T(8,128)S(1)} %dynamic-slice_bitcast_fusion.1), channel_id=1, source_target_pairs={{0,8},{1,9},{2,10},{3,11},{4,12},{5,13},{6,14},{7,15},{8,0},{9,1},... | collective-permute-start | bytes 786440 | tf_op jit(solution)/shard_map/ppermute | solution.py:125
  241.3 9.7 %collective-permute-start.19 = (f32[128,256]{1,0:T(8,128)S(1)}, f32[128,256]{1,0:T(8,128)S(1)}, u32[]{:S(2)}, u32[]{:S(2)}) collective-permute-start(f32[128,256]{1,0:T(8,128)S(1)} %dynamic-slice_bitcast_fusion.4), channel_id=1, source_target_pairs={{0,8},{1,9},{2,10},{3,11},{4,12},{5,13},{6,14},{7,15},{8,0},{9,1},... | collective-permute-start | bytes 393224 | tf_op jit(solution)/shard_map/ppermute | solution.py:125
  249.5 5.0 %collective-permute-start.22 = (f32[128,256]{1,0:T(8,128)S(1)}, f32[128,256]{1,0:T(8,128)S(1)}, u32[]{:S(2)}, u32[]{:S(2)}) collective-permute-start(f32[128,256]{1,0:T(8,128)S(1)} %dynamic-slice_bitcast_fusion.3), channel_id=1, source_target_pairs={{0,2},{1,3},{2,0},{3,1},{4,6},{5,7},{6,4},{7,5},{8,10},{9,11},{10,... | collective-permute-start | bytes 393224 | tf_op jit(solution)/shard_map/ppermute | solution.py:125
  254.6 8.7 %collective-permute-start.23 = (bf16[256,256]{1,0:T(8,128)(2,1)S(1)}, bf16[256,256]{1,0:T(8,128)(2,1)S(1)}, u32[]{:S(2)}, u32[]{:S(2)}) collective-permute-start(bf16[256,256]{1,0:T(8,128)(2,1)S(1)} %fusion.48), channel_id=1, source_target_pairs={{8,16},{9,17},{10,18},{11,19},{12,20},{13,21},{14,22},{15,23},{16,... | collective-permute-start | bytes 393224 | tf_op jit(solution)/shard_map/ppermute | solution.py:136
  (23 other events, 221.1 us)
Sparse Core Ops, SparseCore 0:
  47.3 41.5 all-gather.3
  93.4 40.1 all-gather.5

commit v2 on v1

--- a/solution.py
+++ b/solution.py
@@ -12,6 +12,7 @@
 
 
 rope_base = 500000.0
+wire = jnp.float32
 
 
 def norm_rows(values, gain):
@@ -151,7 +152,21 @@
 
 
 def halve(values, axis, bit, mine):
-    return pick(values, mine, axis) + beside(pick(values, 1 - mine, axis), bit)
+    away = pick(values, 1 - mine, axis).astype(wire)
+    return pick(values, mine, axis) + beside(away, bit).astype(jnp.float32)
+
+
+def grow(values, axis, bit, mine):
+    theirs = beside(values, bit)
+    return jnp.where(
+        mine == 0,
+        jnp.concatenate([values, theirs], axis=axis),
+        jnp.concatenate([theirs, values], axis=axis),
+    )
+
+
+def across_sum(values):
+    return across(values.astype(wire)).astype(jnp.float32)
 
 
 def dot(a, b):
@@ -188,13 +203,23 @@
     rows = slots // ROW_LEN
     blocks = half // block
 
-    normed = norm_rows(stream.astype(jnp.float32), attn_gain).astype(jnp.bfloat16)
-    got = across(lax.dynamic_slice(normed, (core * part, (1 - grp) * half), (part, half)))
+    got = across(lax.dynamic_slice(stream, (core * part, (1 - grp) * half), (part, half)))
     sib = beside(got, 1)
+    wide = stream.astype(jnp.float32)
+    scale = lax.rsqrt(jnp.mean(wide * wide, axis=-1, keepdims=True) + 1e-05)
+    far_scale = across(scale)
+    half_gain = lax.dynamic_slice_in_dim(attn_gain, grp * half, half, 0)
+
+    def scaled(rows_in, factor):
+        return (rows_in.astype(jnp.float32) * factor * half_gain).astype(jnp.bfloat16)
+
+    got = scaled(got, lax.dynamic_slice_in_dim(far_scale, core * part, part, 0))
+    sib = scaled(sib, lax.dynamic_slice_in_dim(far_scale, (1 - core) * part, part, 0))
+    near = scaled(lax.dynamic_slice_in_dim(stream, grp * half, half, 1), scale)
     w_all = jnp.concatenate([w_query, w_key, w_value], axis=1)
     back_got = across(dot(got, w_all))
     back_sib = across(dot(sib, w_all))
-    own = dot(lax.dynamic_slice_in_dim(normed, grp * half, half, 1), w_all)
+    own = dot(near, w_all)
     lo = jnp.where(core == 0, back_got, back_sib)
     hi = jnp.where(core == 0, back_sib, back_got)
     total = own + jnp.concatenate([lo, hi], axis=0)
@@ -240,91 +265,85 @@
     mixed = jnp.einsum("rhqj,rjd->rqhd", probs, vh, preferred_element_type=jnp.float32)
     mixed = mixed.astype(jnp.bfloat16).reshape(slots, block)
 
-    w_out_far = across(after(w_out, back_got, back_sib))
-    all_mixed = lax.all_gather(mixed, "dev", axis=0, tiled=False)
+    z_hi = member // 8
+    place = {8: (0, z_hi), 4: (1, z_lo), 2: (2, y), 1: (3, core)}
+    orders = ((8, 4, 2), (2, 8, 4))
+
+    def spread(rows_in, bits):
+        for bit in bits:
+            rows_in = grow(rows_in, place[bit][0], bit, place[bit][1])
+        return rows_in
 
     def by_blocks(blocked, weight):
         return lax.dot_general(
-            blocked,
+            blocked.reshape(blocks, part, block),
             weight.reshape(blocks, block, -1),
             (((0, 2), (0, 1)), ((), ())),
             preferred_element_type=jnp.float32,
         )
 
-    projected = by_blocks(
-        lax.dynamic_slice_in_dim(all_mixed, grp * blocks, blocks, 0), w_out
-    ) + by_blocks(lax.dynamic_slice_in_dim(all_mixed, (1 - grp) * blocks, blocks, 0), w_out_far)
+    w_out_far = across(after(w_out, back_got, back_sib))
     own_stream = lax.dynamic_slice_in_dim(stream, member * block, block, 1)
-    attended = (own_stream.astype(jnp.float32) + projected).astype(jnp.bfloat16)
-    all_attended = lax.all_gather(attended, "dev", axis=0, tiled=False)
-    far_attended = corner(attended)
-
-    wide = all_attended.astype(jnp.float32)
-    mean = jnp.mean(jnp.mean(wide * wide, axis=2, keepdims=True), axis=0, keepdims=True)
-    normed2 = (
-        wide * lax.rsqrt(mean + 1e-05) * ffn_gain.reshape(members, 1, block)
-    ).astype(jnp.bfloat16)
-    got2 = across(
-        lax.dynamic_slice(normed2, ((1 - grp) * blocks, core * part, 0), (blocks, part, block))
-    )
-    sib2 = beside(got2, 1)
-    gate_got = across(by_blocks(got2, w_gate))
-    up_got = across(by_blocks(got2, w_up))
-    gate_sib = across(by_blocks(sib2, w_gate))
-    up_sib = across(by_blocks(sib2, w_up))
-    near = lax.dynamic_slice_in_dim(normed2, grp * blocks, blocks, 0)
-    near_got = lax.dynamic_slice_in_dim(near, core * part, part, 1)
-    near_sib = lax.dynamic_slice_in_dim(near, (1 - core) * part, part, 1)
-
-    def gated(rows_near, gate_far, up_far):
-        gate = by_blocks(rows_near, w_gate) + gate_far
-        up = by_blocks(rows_near, w_up) + up_far
-        return (jax.nn.silu(gate) * up).astype(jnp.bfloat16)
-
-    hidden_got = gated(near_got, gate_got, up_got)
-    hidden_sib = gated(near_sib, gate_sib, up_sib)
-    far_got = across(hidden_got)
-    far_sib = across(hidden_sib)
-
-    def placed(a, b):
-        lower = jnp.where(core == 0, a, b)
-        upper = jnp.where(core == 0, b, a)
-        return jnp.concatenate([lower, upper], axis=0)
-
-    near_hidden = placed(hidden_got, hidden_sib)
-    far_hidden = placed(far_got, far_sib)
+    gains = ffn_gain.reshape(2, blocks, 1, block)
+    half_gain = pick(gains, grp, 0)
+    attended, near_rows, far_rows = [], [], []
+    for piece, order in enumerate(orders):
+        span = slice(piece * part, (piece + 1) * part)
+        all_mixed = spread(mixed[span].reshape(1, 1, 1, 1, part, block), order + (1,))
+        projected = by_blocks(pick(all_mixed, grp, 0), w_out) + by_blocks(
+            pick(all_mixed, 1 - grp, 0), w_out_far
+        )
+        own = (own_stream[span].astype(jnp.float32) + projected).astype(jnp.bfloat16)
+        attended.append(own)
+        some = spread(own.reshape(1, 1, 1, 1, part, block), order)
+        got = across(pick(some, 1 - grp, 0))
+        full = spread(some, (1,)).reshape(2, blocks, part, block)
+        wide = full.astype(jnp.float32)
+        mean = jnp.mean(jnp.mean(wide * wide, axis=3, keepdims=True), axis=(0, 1))
+        scale = lax.rsqrt(mean + 1e-05)
+        far_scale = across(scale)
+        far = grow(got, 2, 1, core).reshape(blocks, part, block)
+        near = pick(full, grp, 0).astype(jnp.float32)
+        near_rows.append((near * scale * half_gain).astype(jnp.bfloat16))
+        far_rows.append((far.astype(jnp.float32) * far_scale * half_gain).astype(jnp.bfloat16))
+    far_attended = corner(jnp.concatenate(attended, axis=0))
+
+    gate_far, up_far = [], []
+    for far in far_rows:
+        gate_far.append(across_sum(by_blocks(far, w_gate)))
+        up_far.append(across_sum(by_blocks(far, w_up)))
     w_pairs = w_down.reshape(blocks // 2, 2, block, -1)
     w_send = pick(w_pairs, 1 - core, 1)
     w_keep = pick(w_pairs, core, 1)
 
     def down(rows_in, weight):
-        out = dot_t(rows_in, weight.reshape(-1, weight.shape[-1]))
-        return out.reshape(slots, blocks // 2, block)
-
-    def stage(rows_in):
-        return down(rows_in, w_keep) + beside(down(rows_in, w_send), 1)
-
-    near_sum, far_sum = stage(near_hidden), stage(far_hidden)
-
-    def folded(sums):
-        return jnp.moveaxis(sums, 1, 0).reshape(2, 2, slots, block)
-
-    is_near = member // (members // 2) == grp
-    near_sum, far_sum = folded(near_sum), folded(far_sum)
-    keep_all = jnp.stack([near_sum, far_sum])
+        return jnp.stack([dot_t(rows_in, weight[i]) for i in range(blocks // 2)])
+
+    def summed_pairs(rows_in, piece):
+        sums = down(rows_in, w_keep) + beside(down(rows_in, w_send), 1)
+        sums = sums.reshape(2, 2, part, block)
+        if piece == 0:
+            return halve(halve(sums, 1, 2, y), 0, 4, z_lo)
+        return halve(halve(sums, 0, 4, z_lo), 0, 2, y)
+
+    is_near = z_hi == grp
     side = jnp.where(is_near, 0, 1)
-    one, two = keep_all[:, :, :, :part], keep_all[:, :, :, part:]
-    one = halve(one, 2, 2, y)
-    two = halve(two, 1, 4, z_lo)
-    one = halve(one, 1, 4, z_lo)
-    two = halve(two, 0, 8, side)
-    one = halve(one, 0, 8, side)
-    two = halve(two, 0, 2, y)
-    summed = jnp.concatenate([one, two], axis=0)
-    base = jnp.where(is_near, attended, far_attended)
-    done = (base.astype(jnp.float32) + summed).astype(jnp.bfloat16)
-    next_stream = jnp.where(is_near, done, corner(done))
-    return (keys, values, next_stream)
+    near_sums, far_sums = [], []
+    for piece in range(2):
+        gate = by_blocks(near_rows[piece], w_gate) + gate_far[piece]
+        up = by_blocks(near_rows[piece], w_up) + up_far[piece]
+        hidden = (jax.nn.silu(gate) * up).astype(jnp.bfloat16)
+        far_hidden = across(hidden)
+        near_sums.append(summed_pairs(hidden, piece))
+        far_sums.append(summed_pairs(far_hidden, piece))
+    done = []
+    for piece in range(2):
+        span = slice(piece * part, (piece + 1) * part)
+        total = halve(jnp.stack([near_sums[piece], far_sums[piece]]), 0, 8, side)
+        base = jnp.where(is_near, attended[piece], far_attended[span])
+        ours = (base.astype(jnp.float32) + total).astype(jnp.bfloat16)
+        done.append(jnp.where(is_near, ours, corner(ours)))
+    return (keys, values, jnp.concatenate(done, axis=0))
 
 
 def solution(mesh):

time: 271 us -> 224 us (0.83)
  waiting for transfers between devices: 185 us -> 120 us
  starting transfers between devices: 26.8 us -> 58.4 us
  between operations: 14.8 us -> 2.01 us
  local copies, waits for them, and re-layouts: 8.33 us -> 5.59 us
    all_gather x2 -> x0, waiting for transfers between devices: 81.2 us -> none  [the longest x1 40.9 us: moved_rows(): all_mixed = lax.all_gather(mixed, 'dev', axis=0, tiled=False)]
    ppermute x11 -> x34, waiting for transfers between devices: 25.3 us -> 52.3 us  [beside(): return lax.ppermute(values, 'dev', [(i, i ^ bit) for i in range(members)])]
    ppermute x11 -> x34, starting transfers between devices: 11.4 us -> 30.7 us  [beside(): return lax.ppermute(values, 'dev', [(i, i ^ bit) for i in range(members)])]
    ppermute x11 -> x15, waiting for transfers between devices: 73.7 us -> 62 us  [across(): return lax.ppermute(values, 'grp', [(0, 1), (1, 0)])]
    ppermute x2 -> x3, starting transfers between devices: 4.74 us -> 15.2 us  [corner(): return lax.ppermute(values, ('grp', 'dev'), pairs)]
    select_n x4 -> x16, other arithmetic: 1.09 us -> 4.71 us  [the longest x14 4.69 us: grow(): jnp.where(mine == 0, jnp.concatenate([values, theirs], axis=axis), jnp.co...]
    unnamed x47 -> x24, local copies, waits for them, and re-layouts: 5.65 us -> 2.02 us
    dot_general x4 -> x32, matrix products: 6.91 us -> 9.62 us  [dot_t(): lax.dot_general(a, b, (((1,), (1,)), ((), ())), preferred_element_type=jn...]
  transfers between devices with their start and end apart: 26 -> 52, of which waited for: 19 -> 31; matrix products, arithmetic and copies ran while one was open for 9% -> 17% of each run, Pallas kernels for 0% -> 0%
where the time goes in v2:
time: 224 us; the launch traced here: 223 us
  waiting for transfers between devices  120 us (54%)
  starting transfers between devices  58.4 us (26%)
  matrix products  23.4 us (10%)
  other arithmetic  13.8 us (6%)
  local copies, waits for them, and re-layouts  5.59 us (2%)
    ppermute x15, waiting for transfers between devices, across(): return lax.ppermute(values, 'grp', [(0, 1), (1, 0)])  62 us
    ppermute x34, waiting for transfers between devices, beside(): return lax.ppermute(values, 'dev', [(i, i ^ bit) for i in range(members)])  52.3 us
    ppermute x34, starting transfers between devices, beside(): return lax.ppermute(values, 'dev', [(i, i ^ bit) for i in range(members)])  30.7 us
    ppermute x3, starting transfers between devices, corner(): return lax.ppermute(values, ('grp', 'dev'), pairs)  15.2 us
    ppermute x15, starting transfers between devices, across(): return lax.ppermute(values, 'grp', [(0, 1), (1, 0)])  12.5 us
    dot_general x32, matrix products, dot_t(): lax.dot_general(a, b, (((1,), (1,)), ((), ())), preferred_element_type=jn...  9.62 us
    dot_general x12, matrix products, by_blocks(): lax.dot_general(blocked.reshape(blocks, part, block), weight.reshape(bloc...  8.88 us
    ppermute x3, waiting for transfers between devices, corner(): return lax.ppermute(values, ('grp', 'dev'), pairs)  6 us
  transfers between devices with their start and end apart: 52, of which 31 were waited for; matrix products, arithmetic and copies ran while one was open for 17% of the time, Pallas kernels for 0%

profile of v2, /device:TPU:10, one launch (start us, length us, event | category | flops | bytes accessed | tf_op | source)
XLA Modules:
  0.0 223.4 jit_solution(9381828637778558976)
XLA Ops:
  8.1 7.6 %collective-permute-done = bf16[128,2048]{1,0:T(8,128)(2,1)} collective-permute-done((bf16[128,2048]{1,0:T(8,128)(2,1)S(1)}, bf16[128,2048]{1,0:T(8,128)(2,1)}, u32[]{:S(2)}, u32[]{:S(2)}) %collective-permute-start) | collective-permute-done | bytes 524320 | tf_op jit(solution)/shard_map/ppermute | solution.py:121
  22.1 3.8 %collective-permute-done.2 = f32[128,384]{1,0:T(8,128)S(1)} collective-permute-done((f32[128,384]{1,0:T(8,128)S(1)}, f32[128,384]{1,0:T(8,128)S(1)}, u32[]{:S(2)}, u32[]{:S(2)}) %collective-permute-start.2) | collective-permute-done | bytes 196640 | tf_op jit(solution)/shard_map/ppermute | solution.py:121
  25.9 3.8 %collective-permute-done.4 = f32[128,384]{1,0:T(8,128)S(1)} collective-permute-done((f32[128,384]{1,0:T(8,128)S(1)}, f32[128,384]{1,0:T(8,128)S(1)}, u32[]{:S(2)}, u32[]{:S(2)}) %collective-permute-start.4) | collective-permute-done | bytes 196640 | tf_op jit(solution)/shard_map/ppermute | solution.py:121
  36.4 3.0 %collective-permute-done.6 = bf16[1,1,1,1,128,256]{5,4,3,2,1,0:T(8,128)(2,1)S(1)} collective-permute-done((bf16[1,1,1,1,128,256]{5,4,3,2,1,0:T(8,128)(2,1)S(1)}, bf16[1,1,1,1,128,256]{5,4,3,2,1,0:T(8,128)(2,1)S(1)}, u32[]{:S(2)}, u32[]{:S(2)}) %collective-permute-start.6) | collective-permute-done | bytes 65568 | tf_op jit(solution)/shard_map/ppermute | solution.py:126
  47.1 3.4 %collective-permute-start.12 = (bf16[1,1,2,1,128,256]{5,4,3,2,1,0:T(8,128)(2,1)S(1)}, bf16[1,1,2,1,128,256]{5,4,3,2,1,0:T(8,128)(2,1)S(1)}, u32[]{:S(2)}, u32[]{:S(2)}) collective-permute-start(bf16[1,1,2,1,128,256]{5,4,3,2,1,0:T(8,128)(2,1)S(1)} %maximum_select_fusion.20), channel_id=1, source_target_pairs={{0,8},{1,9},{2,10},{3,11},{4,12},{5,13},{6,14},{7,15},{8,0},{9,1},... | collective-permute-start | bytes 393224 | tf_op jit(solution)/shard_map/ppermute | solution.py:126
  57.0 6.4 %collective-permute-done.13 = bf16[2,1,2,1,128,256]{5,4,3,2,1,0:T(8,128)(2,1)} collective-permute-done((bf16[2,1,2,1,128,256]{5,4,3,2,1,0:T(8,128)(2,1)}, bf16[2,1,2,1,128,256]{5,4,3,2,1,0:T(8,128)(2,1)}, u32[]{:S(2)}, u32[]{:S(2)}) %collective-permute-start.13) | collective-permute-done | bytes 262176 | tf_op jit(solution)/shard_map/ppermute | solution.py:126
  66.4 4.0 %collective-permute-done.10 = bf16[2048,256]{1,0:T(8,128)(2,1)S(1)} collective-permute-done((bf16[2048,256]{1,0:T(8,128)(2,1)S(1)}, bf16[2048,256]{1,0:T(8,128)(2,1)S(1)}, u32[]{:S(2)}, u32[]{:S(2)}) %collective-permute-start.10) | collective-permute-done | bytes 1048608 | tf_op jit(solution)/shard_map/ppermute | solution.py:121
  71.5 3.4 %collective-permute-start.16 = (bf16[1,1,1,1,128,256]{5,4,3,2,1,0:T(8,128)(2,1)S(1)}, bf16[1,1,1,1,128,256]{5,4,3,2,1,0:T(8,128)(2,1)S(1)}, u32[]{:S(2)}, u32[]{:S(2)}) collective-permute-start(bf16[1,1,1,1,128,256]{5,4,3,2,1,0:T(8,128)(2,1)S(1)} %bitcast.494), channel_id=1, source_target_pairs={{0,8},{1,9},{2,10},{3,11},{4,12},{5,13},{6,14},{7,15},{8,0},{9,1},... | collective-permute-start | bytes 196616 | tf_op jit(solution)/shard_map/ppermute | solution.py:126
  78.0 3.0 %collective-permute-done.34 = bf16[1,1,1,1,128,256]{5,4,3,2,1,0:T(8,128)(2,1)S(1)} collective-permute-done((bf16[1,1,1,1,128,256]{5,4,3,2,1,0:T(8,128)(2,1)S(1)}, bf16[1,1,1,1,128,256]{5,4,3,2,1,0:T(8,128)(2,1)S(1)}, u32[]{:S(2)}, u32[]{:S(2)}) %collective-permute-start.34) | collective-permute-done | bytes 65568 | tf_op jit(solution)/shard_map/ppermute | solution.py:126
  84.0 4.4 %collective-permute-done.35 = bf16[1,1,2,1,128,256]{5,4,3,2,1,0:T(8,128)(2,1)S(1)} collective-permute-done((bf16[1,1,2,1,128,256]{5,4,3,2,1,0:T(8,128)(2,1)S(1)}, bf16[1,1,2,1,128,256]{5,4,3,2,1,0:T(8,128)(2,1)S(1)}, u32[]{:S(2)}, u32[]{:S(2)}) %collective-permute-start.35) | collective-permute-done | bytes 131104 | tf_op jit(solution)/shard_map/ppermute | solution.py:126
  90.3 4.5 %collective-permute-done.36 = bf16[2,1,2,1,128,256]{5,4,3,2,1,0:T(8,128)(2,1)S(1)} collective-permute-done((bf16[2,1,2,1,128,256]{5,4,3,2,1,0:T(8,128)(2,1)S(1)}, bf16[2,1,2,1,128,256]{5,4,3,2,1,0:T(8,128)(2,1)S(1)}, u32[]{:S(2)}, u32[]{:S(2)}) %collective-permute-start.36) | collective-permute-done | bytes 262176 | tf_op jit(solution)/shard_map/ppermute | solution.py:126
  98.9 5.2 %collective-permute-done.38 = bf16[2,2,1,128,256]{4,3,1,0,2:T(8,128)(2,1)S(1)} collective-permute-done((bf16[2,2,1,128,256]{4,3,1,0,2:T(8,128)(2,1)}, bf16[2,2,1,128,256]{4,3,1,0,2:T(8,128)(2,1)S(1)}, u32[]{:S(2)}, u32[]{:S(2)}) %collective-permute-start.38) | collective-permute-done | bytes 262176 | tf_op jit(solution)/shard_map/ppermute | solution.py:121
  108.4 6.6 %collective-permute-start.15 = (bf16[256,256]{1,0:T(8,128)(2,1)S(1)}, bf16[256,256]{1,0:T(8,128)(2,1)S(1)}, u32[]{:S(2)}, u32[]{:S(2)}) collective-permute-start(bf16[256,256]{1,0:T(8,128)(2,1)S(1)} %pad_maximum_fusion.9), channel_id=1, source_target_pairs={{8,16},{9,17},{10,18},{11,19},{12,20},{13,21},{14,22},{15,23},{16,... | collective-permute-start | bytes 393224 | tf_op jit(solution)/shard_map/ppermute | solution.py:137
  122.6 7.1 %collective-permute-done.23 = f32[128,896]{1,0:T(8,128)S(1)} collective-permute-done((f32[128,896]{1,0:T(8,128)S(1)}, f32[128,896]{1,0:T(8,128)S(1)}, u32[]{:S(2)}, u32[]{:S(2)}) %collective-permute-start.23) | collective-permute-done | bytes 458784 | tf_op jit(solution)/shard_map/ppermute | solution.py:121
  130.4 9.0 %collective-permute-done.24 = f32[128,896]{1,0:T(8,128)S(1)} collective-permute-done((f32[128,896]{1,0:T(8,128)S(1)}, f32[128,896]{1,0:T(8,128)S(1)}, u32[]{:S(2)}, u32[]{:S(2)}) %collective-permute-start.24) | collective-permute-done | bytes 458784 | tf_op jit(solution)/shard_map/ppermute | solution.py:121
  142.8 6.5 %collective-permute-done.41 = f32[128,896]{1,0:T(8,128)S(1)} collective-permute-done((f32[128,896]{1,0:T(8,128)S(1)}, f32[128,896]{1,0:T(8,128)S(1)}, u32[]{:S(2)}, u32[]{:S(2)}) %collective-permute-start.41) | collective-permute-done | bytes 458784 | tf_op jit(solution)/shard_map/ppermute | solution.py:121
  150.1 9.1 %collective-permute-done.42 = f32[128,896]{1,0:T(8,128)S(1)} collective-permute-done((f32[128,896]{1,0:T(8,128)S(1)}, f32[128,896]{1,0:T(8,128)S(1)}, u32[]{:S(2)}, u32[]{:S(2)}) %collective-permute-start.42) | collective-permute-done | bytes 458784 | tf_op jit(solution)/shard_map/ppermute | solution.py:121
  164.8 3.0 %collective-permute-done.46 = bf16[128,896]{1,0:T(8,128)(2,1)S(1)} collective-permute-done((bf16[128,896]{1,0:T(8,128)(2,1)S(1)}, bf16[128,896]{1,0:T(8,128)(2,1)S(1)}, u32[]{:S(2)}, u32[]{:S(2)}) %collective-permute-start.46) | collective-permute-done | bytes 229408 | tf_op jit(solution)/shard_map/ppermute | solution.py:121
  176.5 4.5 %collective-permute-done.26 = f32[2,128,256]{2,1,0:T(8,128)S(1)} collective-permute-done((f32[2,128,256]{2,1,0:T(8,128)S(1)}, f32[2,128,256]{2,1,0:T(8,128)S(1)}, u32[]{:S(2)}, u32[]{:S(2)}) %collective-permute-start.26) | collective-permute-done | bytes 262176 | tf_op jit(solution)/shard_map/ppermute | solution.py:126
  183.3 6.3 %collective-permute-done.27 = f32[128,256]{1,0:T(8,128)S(1)} collective-permute-done((f32[128,256]{1,0:T(8,128)S(1)}, f32[128,256]{1,0:T(8,128)S(1)}, u32[]{:S(2)}, u32[]{:S(2)}) %collective-permute-start.27) | collective-permute-done | bytes 131104 | tf_op jit(solution)/shard_map/ppermute | solution.py:126
  192.0 2.9 %collective-permute-done.31 = f32[128,256]{1,0:T(8,128)S(1)} collective-permute-done((f32[128,256]{1,0:T(8,128)S(1)}, f32[128,256]{1,0:T(8,128)S(1)}, u32[]{:S(2)}, u32[]{:S(2)}) %collective-permute-start.31) | collective-permute-done | bytes 131104 | tf_op jit(solution)/shard_map/ppermute | solution.py:126
  198.0 6.2 %collective-permute-done.32 = f32[128,256]{1,0:T(8,128)S(1)} collective-permute-done((f32[128,256]{1,0:T(8,128)S(1)}, f32[128,256]{1,0:T(8,128)S(1)}, u32[]{:S(2)}, u32[]{:S(2)}) %collective-permute-start.32) | collective-permute-done | bytes 131104 | tf_op jit(solution)/shard_map/ppermute | solution.py:126
  206.5 6.8 %collective-permute-start.51 = (bf16[128,256]{1,0:T(8,128)(2,1)S(1)}, bf16[128,256]{1,0:T(8,128)(2,1)S(1)}, u32[]{:S(2)}, u32[]{:S(2)}) collective-permute-start(bf16[128,256]{1,0:T(8,128)(2,1)S(1)} %get-tuple-element.30), channel_id=1, source_target_pairs={{8,16},{9,17},{10,18},{11,19},{12,20},{13,21},{14,22},{15,23},{16,... | collective-permute-start | bytes 196616 | tf_op jit(solution)/shard_map/ppermute | solution.py:137
  216.7 6.0 %collective-permute-done.33 = bf16[128,256]{1,0:T(8,128)(2,1)S(1)} collective-permute-done((bf16[128,256]{1,0:T(8,128)(2,1)S(1)}, bf16[128,256]{1,0:T(8,128)(2,1)S(1)}, u32[]{:S(2)}, u32[]{:S(2)}) %collective-permute-start.33) | collective-permute-done | bytes 65568 | tf_op jit(solution)/shard_map/ppermute | solution.py:137
  (254 shorter events, 94.8 us)
Async XLA Ops:
  1.9 13.8 %collective-permute-start = (bf16[128,2048]{1,0:T(8,128)(2,1)S(1)}, bf16[128,2048]{1,0:T(8,128)(2,1)}, u32[]{:S(2)}, u32[]{:S(2)}) collective-permute-start(bf16[128,2048]{1,0:T(8,128)(2,1)S(1)} %dynamic_slice.128), channel_id=1, source_target_pairs={{0,16},{16,0},{1,17},{17,1},{2,18},{18,2},{3,19},{19,3},{4,20},{20... | collective-permute-start | bytes 1572872 | tf_op jit(solution)/shard_map/ppermute | solution.py:121
  4.6 11.8 %collective-permute-start.1 = (f32[256,1]{0,1:T(1,128)S(1)}, f32[256,1]{0,1:T(1,128)S(1)}, u32[]{:S(2)}, u32[]{:S(2)}) collective-permute-start(f32[256,1]{0,1:T(1,128)S(1)} %bitcast.524), channel_id=1, source_target_pairs={{0,16},{16,0},{1,17},{17,1},{2,18},{18,2},{3,19},{19,3},{4,20},{20... | collective-permute-start | bytes 3080 | tf_op jit(solution)/shard_map/ppermute | solution.py:121
  20.4 9.3 %collective-permute-start.4 = (f32[128,384]{1,0:T(8,128)S(1)}, f32[128,384]{1,0:T(8,128)S(1)}, u32[]{:S(2)}, u32[]{:S(2)}) collective-permute-start(f32[128,384]{1,0:T(8,128)S(1)} %fusion.22), channel_id=1, source_target_pairs={{0,16},{16,0},{1,17},{17,1},{2,18},{18,2},{3,19},{19,3},{4,20},{20... | collective-permute-start | bytes 589832 | tf_op jit(solution)/shard_map/ppermute | solution.py:121
  46.5 23.9 %collective-permute-start.10 = (bf16[2048,256]{1,0:T(8,128)(2,1)S(1)}, bf16[2048,256]{1,0:T(8,128)(2,1)S(1)}, u32[]{:S(2)}, u32[]{:S(2)}) collective-permute-start(bf16[2048,256]{1,0:T(8,128)(2,1)S(1)} %copy-done.3), channel_id=1, source_target_pairs={{0,16},{16,0},{1,17},{17,1},{2,18},{18,2},{3,19},{19,3},{4,20},{20... | collective-permute-start | bytes 3145736 | tf_op jit(solution)/shard_map/ppermute | solution.py:121
  53.5 11.1 %collective-permute-start.9 = (bf16[2,2,2,1,128,256]{5,4,3,2,1,0:T(8,128)(2,1)S(1)}, bf16[2,2,2,1,128,256]{5,4,3,2,1,0:T(8,128)(2,1)}, u32[]{:S(2)}, u32[]{:S(2)}) collective-permute-start(bf16[2,2,2,1,128,256]{5,4,3,2,1,0:T(8,128)(2,1)S(1)} %maximum_select_fusion.4), channel_id=1, source_target_pairs={{0,1},{1,0},{2,3},{3,2},{4,5},{5,4},{6,7},{7,6},{8,9},{9,8},{10,11... | collective-permute-start | bytes 1572872 | tf_op jit(solution)/shard_map/ppermute | solution.py:126
  64.5 10.5 %collective-permute-start.14 = (bf16[2,2,2,1,128,256]{5,4,3,2,1,0:T(8,128)(2,1)S(1)}, bf16[2,2,2,1,128,256]{5,4,3,2,1,0:T(8,128)(2,1)S(1)}, u32[]{:S(2)}, u32[]{:S(2)}) collective-permute-start(bf16[2,2,2,1,128,256]{5,4,3,2,1,0:T(8,128)(2,1)S(1)} %maximum_select_fusion.5), channel_id=1, source_target_pairs={{0,1},{1,0},{2,3},{3,2},{4,5},{5,4},{6,7},{7,6},{8,9},{9,8},{10,11... | collective-permute-start | bytes 1572872 | tf_op jit(solution)/shard_map/ppermute | solution.py:126
  89.6 14.5 %collective-permute-start.19 = (bf16[2,2,2,1,128,256]{5,4,3,2,1,0:T(8,128)(2,1)S(1)}, bf16[2,2,2,1,128,256]{5,4,3,2,1,0:T(8,128)(2,1)S(1)}, u32[]{:S(2)}, u32[]{:S(2)}) collective-permute-start(bf16[2,2,2,1,128,256]{5,4,3,2,1,0:T(8,128)(2,1)S(1)} %maximum_select_fusion.6), channel_id=1, source_target_pairs={{0,1},{1,0},{2,3},{3,2},{4,5},{5,4},{6,7},{7,6},{8,9},{9,8},{10,11... | collective-permute-start | bytes 1572872 | tf_op jit(solution)/shard_map/ppermute | solution.py:126
  98.9 16.1 %collective-permute-start.21 = (bf16[2,2,1,128,256]{4,3,1,0,2:T(8,128)(2,1)S(1)}, bf16[2,2,1,128,256]{4,3,1,0,2:T(8,128)(2,1)S(1)}, u32[]{:S(2)}, u32[]{:S(2)}) collective-permute-start(bf16[2,2,1,128,256]{4,3,1,0,2:T(8,128)(2,1)S(1)} %bitcast.504), channel_id=1, source_target_pairs={{0,1},{1,0},{2,3},{3,2},{4,5},{5,4},{6,7},{7,6},{8,9},{9,8},{10,11... | collective-permute-start | bytes 786440 | tf_op jit(solution)/shard_map/ppermute | solution.py:126
  104.1 10.9 %collective-permute-start.39 = (bf16[2,2,1,128,256]{4,3,1,0,2:T(8,128)(2,1)S(1)}, bf16[2,2,1,128,256]{4,3,1,0,2:T(8,128)(2,1)S(1)}, u32[]{:S(2)}, u32[]{:S(2)}) collective-permute-start(bf16[2,2,1,128,256]{4,3,1,0,2:T(8,128)(2,1)S(1)} %collective-permute-done.38), channel_id=1, source_target_pairs={{0,1},{1,0},{2,3},{3,2},{4,5},{5,4},{6,7},{7,6},{8,9},{9,8},{10,11... | collective-permute-start | bytes 786440 | tf_op jit(solution)/shard_map/ppermute | solution.py:126
  104.5 10.4 %collective-permute-start.22 = (f32[128,1]{0,1:T(1,128)S(1)}, f32[128,1]{0,1:T(1,128)S(1)}, u32[]{:S(2)}, u32[]{:S(2)}) collective-permute-start(f32[128,1]{0,1:T(1,128)S(1)} %get-tuple-element.52), channel_id=1, source_target_pairs={{0,16},{16,0},{1,17},{17,1},{2,18},{18,2},{3,19},{19,3},{4,20},{20... | collective-permute-start | bytes 1544 | tf_op jit(solution)/shard_map/ppermute | solution.py:121
  108.4 89.7 %collective-permute-start.15 = (bf16[256,256]{1,0:T(8,128)(2,1)S(1)}, bf16[256,256]{1,0:T(8,128)(2,1)S(1)}, u32[]{:S(2)}, u32[]{:S(2)}) collective-permute-start(bf16[256,256]{1,0:T(8,128)(2,1)S(1)} %pad_maximum_fusion.9), channel_id=1, source_target_pairs={{8,16},{9,17},{10,18},{11,19},{12,20},{13,21},{14,22},{15,23},{16,... | collective-permute-start | bytes 393224 | tf_op jit(solution)/shard_map/ppermute | solution.py:137
  116.1 13.5 %collective-permute-start.23 = (f32[128,896]{1,0:T(8,128)S(1)}, f32[128,896]{1,0:T(8,128)S(1)}, u32[]{:S(2)}, u32[]{:S(2)}) collective-permute-start(f32[128,896]{1,0:T(8,128)S(1)} %convolution_bitcast_fusion.6), channel_id=1, source_target_pairs={{0,16},{16,0},{1,17},{17,1},{2,18},{18,2},{3,19},{19,3},{4,20},{20... | collective-permute-start | bytes 1376264 | tf_op jit(solution)/shard_map/ppermute | solution.py:121
  117.0 22.5 %collective-permute-start.24 = (f32[128,896]{1,0:T(8,128)S(1)}, f32[128,896]{1,0:T(8,128)S(1)}, u32[]{:S(2)}, u32[]{:S(2)}) collective-permute-start(f32[128,896]{1,0:T(8,128)S(1)} %convolution_bitcast_fusion.4), channel_id=1, source_target_pairs={{0,16},{16,0},{1,17},{17,1},{2,18},{18,2},{3,19},{19,3},{4,20},{20... | collective-permute-start | bytes 1376264 | tf_op jit(solution)/shard_map/ppermute | solution.py:121
  120.5 28.8 %collective-permute-start.41 = (f32[128,896]{1,0:T(8,128)S(1)}, f32[128,896]{1,0:T(8,128)S(1)}, u32[]{:S(2)}, u32[]{:S(2)}) collective-permute-start(f32[128,896]{1,0:T(8,128)S(1)} %convolution_bitcast_fusion.2), channel_id=1, source_target_pairs={{0,16},{16,0},{1,17},{17,1},{2,18},{18,2},{3,19},{19,3},{4,20},{20... | collective-permute-start | bytes 1376264 | tf_op jit(solution)/shard_map/ppermute | solution.py:121
  120.6 38.6 %collective-permute-start.42 = (f32[128,896]{1,0:T(8,128)S(1)}, f32[128,896]{1,0:T(8,128)S(1)}, u32[]{:S(2)}, u32[]{:S(2)}) collective-permute-start(f32[128,896]{1,0:T(8,128)S(1)} %convolution_bitcast_fusion), channel_id=1, source_target_pairs={{0,16},{16,0},{1,17},{17,1},{2,18},{18,2},{3,19},{19,3},{4,20},{20... | collective-permute-start | bytes 1376264 | tf_op jit(solution)/shard_map/ppermute | solution.py:121
  141.8 21.7 %collective-permute-start.28 = (bf16[128,896]{1,0:T(8,128)(2,1)S(1)}, bf16[128,896]{1,0:T(8,128)(2,1)S(1)}, u32[]{:S(2)}, u32[]{:S(2)}) collective-permute-start(bf16[128,896]{1,0:T(8,128)(2,1)S(1)} %multiply_convert_fusion.10), channel_id=1, source_target_pairs={{0,16},{16,0},{1,17},{17,1},{2,18},{18,2},{3,19},{19,3},{4,20},{20... | collective-permute-start | bytes 688136 | tf_op jit(solution)/shard_map/ppermute | solution.py:121
  161.9 9.8 %collective-permute-start.25 = (f32[4,128,256]{2,1,0:T(8,128)S(1)}, f32[4,128,256]{2,1,0:T(8,128)S(1)}, u32[]{:S(2)}, u32[]{:S(2)}) collective-permute-start(f32[4,128,256]{2,1,0:T(8,128)S(1)} %pad_maximum_fusion.3), channel_id=1, source_target_pairs={{0,1},{1,0},{2,3},{3,2},{4,5},{5,4},{6,7},{7,6},{8,9},{9,8},{10,11... | collective-permute-start | bytes 1572872 | tf_op jit(solution)/shard_map/ppermute | solution.py:126
  162.0 10.6 %collective-permute-start.43 = (f32[4,128,256]{2,1,0:T(8,128)S(1)}, f32[4,128,256]{2,1,0:T(8,128)S(1)}, u32[]{:S(2)}, u32[]{:S(2)}) collective-permute-start(f32[4,128,256]{2,1,0:T(8,128)S(1)} %pad_maximum_fusion.5), channel_id=1, source_target_pairs={{0,1},{1,0},{2,3},{3,2},{4,5},{5,4},{6,7},{7,6},{8,9},{9,8},{10,11... | collective-permute-start | bytes 1572872 | tf_op jit(solution)/shard_map/ppermute | solution.py:126
  172.8 9.2 %collective-permute-start.44 = (f32[2,128,256]{2,1,0:T(8,128)S(1)}, f32[2,128,256]{2,1,0:T(8,128)S(1)}, u32[]{:S(2)}, u32[]{:S(2)}) collective-permute-start(f32[2,128,256]{2,1,0:T(8,128)S(1)} %dynamic-slice_bitcast_fusion.41), channel_id=1, source_target_pairs={{0,4},{1,5},{2,6},{3,7},{4,0},{5,1},{6,2},{7,3},{8,12},{9,13},{10,... | collective-permute-start | bytes 786440 | tf_op jit(solution)/shard_map/ppermute | solution.py:126
  173.7 16.0 %collective-permute-start.30 = (f32[2,128,256]{2,1,0:T(8,128)S(1)}, f32[2,128,256]{2,1,0:T(8,128)S(1)}, u32[]{:S(2)}, u32[]{:S(2)}) collective-permute-start(f32[2,128,256]{2,1,0:T(8,128)S(1)} %dynamic-slice_bitcast_fusion.43), channel_id=1, source_target_pairs={{0,2},{1,3},{2,0},{3,1},{4,6},{5,7},{6,4},{7,5},{8,10},{9,11},{10,... | collective-permute-start | bytes 786440 | tf_op jit(solution)/shard_map/ppermute | solution.py:126
  175.1 15.6 %collective-permute-start.48 = (f32[2,128,256]{2,1,0:T(8,128)S(1)}, f32[2,128,256]{2,1,0:T(8,128)S(1)}, u32[]{:S(2)}, u32[]{:S(2)}) collective-permute-start(f32[2,128,256]{2,1,0:T(8,128)S(1)} %dynamic-slice_bitcast_fusion.40), channel_id=1, source_target_pairs={{0,4},{1,5},{2,6},{3,7},{4,0},{5,1},{6,2},{7,3},{8,12},{9,13},{10,... | collective-permute-start | bytes 786440 | tf_op jit(solution)/shard_map/ppermute | solution.py:126
  194.9 9.3 %collective-permute-start.32 = (f32[128,256]{1,0:T(8,128)S(1)}, f32[128,256]{1,0:T(8,128)S(1)}, u32[]{:S(2)}, u32[]{:S(2)}) collective-permute-start(f32[128,256]{1,0:T(8,128)S(1)} %fusion.44), channel_id=1, source_target_pairs={{0,8},{1,9},{2,10},{3,11},{4,12},{5,13},{6,14},{7,15},{8,0},{9,1},... | collective-permute-start | bytes 393224 | tf_op jit(solution)/shard_map/ppermute | solution.py:126
  196.9 9.5 %collective-permute-start.50 = (f32[128,256]{1,0:T(8,128)S(1)}, f32[128,256]{1,0:T(8,128)S(1)}, u32[]{:S(2)}, u32[]{:S(2)}) collective-permute-start(f32[128,256]{1,0:T(8,128)S(1)} %fusion.37), channel_id=1, source_target_pairs={{0,8},{1,9},{2,10},{3,11},{4,12},{5,13},{6,14},{7,15},{8,0},{9,1},... | collective-permute-start | bytes 393224 | tf_op jit(solution)/shard_map/ppermute | solution.py:126
  206.5 10.2 %collective-permute-start.51 = (bf16[128,256]{1,0:T(8,128)(2,1)S(1)}, bf16[128,256]{1,0:T(8,128)(2,1)S(1)}, u32[]{:S(2)}, u32[]{:S(2)}) collective-permute-start(bf16[128,256]{1,0:T(8,128)(2,1)S(1)} %get-tuple-element.30), channel_id=1, source_target_pairs={{8,16},{9,17},{10,18},{11,19},{12,20},{13,21},{14,22},{15,23},{16,... | collective-permute-start | bytes 196616 | tf_op jit(solution)/shard_map/ppermute | solution.py:137
  (38 other events, 332.4 us)

commit v3 on v2

--- a/solution.py
+++ b/solution.py
@@ -1,8 +1,11 @@
+import functools
 import math
 
 import jax
 import jax.numpy as jnp
 from jax import lax
+from jax.experimental import pallas as pl
+from jax.experimental.pallas import tpu as pltpu
 from jax.sharding import PartitionSpec as P
 
 HEADS = 32
@@ -156,15 +159,6 @@
     return pick(values, mine, axis) + beside(away, bit).astype(jnp.float32)
 
 
-def grow(values, axis, bit, mine):
-    theirs = beside(values, bit)
-    return jnp.where(
-        mine == 0,
-        jnp.concatenate([values, theirs], axis=axis),
-        jnp.concatenate([theirs, values], axis=axis),
-    )
-
-
 def across_sum(values):
     return across(values.astype(wire)).astype(jnp.float32)
 
@@ -175,6 +169,124 @@
 
 def dot_t(a, b):
     return lax.dot_general(a, b, (((1,), (1,)), ((), ())), preferred_element_type=jnp.float32)
+
+
+link_orders = ((8, 4, 2, 1), (2, 8, 4, 1))
+
+
+def flipped(index, bits):
+    for bit in (8, 4, 2, 1):
+        if bits & bit:
+            index = index + bit * (1 - 2 * (index // bit % 2))
+    return index
+
+
+def subsets(bits):
+    found = [0]
+    for bit in bits:
+        found = found + [have | bit for have in found]
+    return found
+
+
+def spread_kernel(both_groups, src_ref, out_ref, *rest):
+    if both_groups:
+        far_ref, send_sem, recv_sem, far_send, far_recv = rest
+    else:
+        send_sem, recv_sem = rest
+    grp, me = lax.axis_index("grp"), lax.axis_index("dev")
+    core = me % 2
+    barrier = pltpu.get_barrier_semaphore()
+    targets = [{"dev": flipped(me, bit)} for bit in (8, 4, 2, 1)]
+    if both_groups:
+        targets.append({"grp": 1 - grp})
+    for target in targets:
+        pl.semaphore_signal(
+            barrier, inc=1, device_id=target, device_id_type=pl.DeviceIdType.MESH
+        )
+    pl.semaphore_wait(barrier, len(targets))
+
+    pieces = len(link_orders)
+    copies, far_copies, near_copies = {}, {}, {}
+
+    def copy_to(source, target, sent, arrived):
+        copy = pltpu.make_async_remote_copy(
+            src_ref=source,
+            dst_ref=target[0],
+            send_sem=sent,
+            recv_sem=arrived,
+            device_id=target[1],
+            device_id_type=pl.DeviceIdType.MESH,
+        )
+        copy.start()
+        return copy
+
+    def forward(piece, have):
+        order = link_orders[piece]
+        later = 1 + max([order.index(bit) for bit in order if have & bit], default=-1)
+        block = out_ref.at[piece, flipped(me, have)]
+        for bit in order[later:]:
+            index = have | bit
+            copies[piece, index] = copy_to(
+                block,
+                (block, {"dev": flipped(me, bit)}),
+                send_sem.at[piece, index],
+                recv_sem.at[piece, index],
+            )
+
+    for piece in range(pieces):
+        out_ref[piece, me] = src_ref[piece]
+    for piece in range(pieces):
+        forward(piece, 0)
+    for level in range(4):
+        for piece in range(pieces):
+            order = link_orders[piece]
+            for have in subsets(order[:level]):
+                copies[piece, have | order[level]].wait_recv()
+                forward(piece, have | order[level])
+            if both_groups and level == 2:
+                for i in range(4):
+                    far_copies[piece, i] = copy_to(
+                        out_ref.at[piece, (1 - grp) * 8 + i * 2 + core],
+                        (far_ref.at[piece, i * 2 + core], {"grp": 1 - grp}),
+                        far_send.at[piece, i],
+                        far_recv.at[piece, i],
+                    )
+    if both_groups:
+        for piece in range(pieces):
+            for i in range(4):
+                far_copies[piece, i].wait_recv()
+                block = far_ref.at[piece, i * 2 + core]
+                near_copies[piece, i] = copy_to(
+                    block,
+                    (block, {"dev": flipped(me, 1)}),
+                    far_send.at[piece, 4 + i],
+                    far_recv.at[piece, 4 + i],
+                )
+        for copy in near_copies.values():
+            copy.wait_recv()
+    for group in (copies, far_copies, near_copies):
+        for copy in group.values():
+            copy.wait_send()
+
+
+def spread(halves, both_groups, collective):
+    pieces, part, block = halves.shape
+    shapes = [jax.ShapeDtypeStruct((pieces, 16, part, block), halves.dtype)]
+    scratch = [pltpu.SemaphoreType.DMA((pieces, 16)), pltpu.SemaphoreType.DMA((pieces, 16))]
+    if both_groups:
+        shapes.append(jax.ShapeDtypeStruct((pieces, 8, part, block), halves.dtype))
+        scratch += [pltpu.SemaphoreType.DMA((pieces, 8)), pltpu.SemaphoreType.DMA((pieces, 8))]
+    spec = pl.BlockSpec(memory_space=pltpu.VMEM)
+    return pl.pallas_call(
+        functools.partial(spread_kernel, both_groups),
+        out_shape=tuple(shapes),
+        in_specs=[spec],
+        out_specs=tuple(spec for _ in shapes),
+        scratch_shapes=scratch,
+        compiler_params=pltpu.CompilerParams(
+            collective_id=collective, has_side_effects=True, vmem_limit_bytes=16 * 2**20
+        ),
+    )(halves)
 
 
 def moved_rows(
@@ -266,14 +378,6 @@
     mixed = mixed.astype(jnp.bfloat16).reshape(slots, block)
 
     z_hi = member // 8
-    place = {8: (0, z_hi), 4: (1, z_lo), 2: (2, y), 1: (3, core)}
-    orders = ((8, 4, 2), (2, 8, 4))
-
-    def spread(rows_in, bits):
-        for bit in bits:
-            rows_in = grow(rows_in, place[bit][0], bit, place[bit][1])
-        return rows_in
-
     def by_blocks(blocked, weight):
         return lax.dot_general(
             blocked.reshape(blocks, part, block),
@@ -286,27 +390,28 @@
     own_stream = lax.dynamic_slice_in_dim(stream, member * block, block, 1)
     gains = ffn_gain.reshape(2, blocks, 1, block)
     half_gain = pick(gains, grp, 0)
-    attended, near_rows, far_rows = [], [], []
-    for piece, order in enumerate(orders):
+    (all_mixed,) = spread(mixed.reshape(2, part, block), False, 0)
+    all_mixed = all_mixed.reshape(2, 2, blocks, part, block)
+    attended = []
+    for piece in range(2):
         span = slice(piece * part, (piece + 1) * part)
-        all_mixed = spread(mixed[span].reshape(1, 1, 1, 1, part, block), order + (1,))
-        projected = by_blocks(pick(all_mixed, grp, 0), w_out) + by_blocks(
-            pick(all_mixed, 1 - grp, 0), w_out_far
+        projected = by_blocks(pick(all_mixed[piece], grp, 0), w_out) + by_blocks(
+            pick(all_mixed[piece], 1 - grp, 0), w_out_far
         )
-        own = (own_stream[span].astype(jnp.float32) + projected).astype(jnp.bfloat16)
-        attended.append(own)
-        some = spread(own.reshape(1, 1, 1, 1, part, block), order)
-        got = across(pick(some, 1 - grp, 0))
-        full = spread(some, (1,)).reshape(2, blocks, part, block)
-        wide = full.astype(jnp.float32)
-        mean = jnp.mean(jnp.mean(wide * wide, axis=3, keepdims=True), axis=(0, 1))
-        scale = lax.rsqrt(mean + 1e-05)
-        far_scale = across(scale)
-        far = grow(got, 2, 1, core).reshape(blocks, part, block)
-        near = pick(full, grp, 0).astype(jnp.float32)
-        near_rows.append((near * scale * half_gain).astype(jnp.bfloat16))
-        far_rows.append((far.astype(jnp.float32) * far_scale * half_gain).astype(jnp.bfloat16))
-    far_attended = corner(jnp.concatenate(attended, axis=0))
+        attended.append((own_stream[span].astype(jnp.float32) + projected).astype(jnp.bfloat16))
+    all_attended, far_rows_in = spread(jnp.stack(attended), True, 1)
+    near_rows, far_rows = [], []
+    wide = all_attended.astype(jnp.float32)
+    mean = jnp.mean(jnp.mean(wide * wide, axis=3, keepdims=True), axis=1)
+    scales = lax.rsqrt(mean + 1e-05)
+    far_scales = across(scales)
+    for piece in range(2):
+        near = pick(all_attended[piece].reshape(2, blocks, part, block), grp, 0)
+        near = near.astype(jnp.float32) * scales[piece] * half_gain
+        far = far_rows_in[piece].astype(jnp.float32) * far_scales[piece] * half_gain
+        near_rows.append(near.astype(jnp.bfloat16))
+        far_rows.append(far.astype(jnp.bfloat16))
+    far_attended = corner(after(jnp.concatenate(attended, axis=0), *far_rows))
 
     gate_far, up_far = [], []
     for far in far_rows:

time: 224 us -> 210 us (0.938)
  Pallas kernels: 0 us -> 47.7 us
  waiting for transfers between devices: 120 us -> 85.4 us
  starting transfers between devices: 58.4 us -> 38.7 us
  other arithmetic: 13.8 us -> 7.14 us
    pallas_call x0 -> x2, Pallas kernels: none -> 47.7 us  [spread(): pl.pallas_call(functools.partial(spread_kernel, both_groups), out_shape=t...]
    ppermute x34 -> x16, waiting for transfers between devices: 52.3 us -> 18.7 us  [beside(): return lax.ppermute(values, 'dev', [(i, i ^ bit) for i in range(members)])]
    ppermute x34 -> x16, starting transfers between devices: 30.7 us -> 15.8 us  [beside(): return lax.ppermute(values, 'dev', [(i, i ^ bit) for i in range(members)])]
    select_n x14 -> x0, other arithmetic: 4.69 us -> none  [grow(): jnp.where(mine == 0, jnp.concatenate([values, theirs], axis=axis), jnp.co...]
    ppermute x3, starting transfers between devices: 15.2 us -> 12.6 us  [corner(): return lax.ppermute(values, ('grp', 'dev'), pairs)]
    ppermute x15 -> x12, starting transfers between devices: 12.5 us -> 10.3 us  [across(): return lax.ppermute(values, 'grp', [(0, 1), (1, 0)])]
    ppermute x15 -> x12, waiting for transfers between devices: 62 us -> 60.6 us  [across(): return lax.ppermute(values, 'grp', [(0, 1), (1, 0)])]
  transfers between devices with their start and end apart: 52 -> 31, of which waited for: 31 -> 17; matrix products, arithmetic and copies ran while one was open for 17% -> 13% of each run, Pallas kernels for 0% -> 9%
where the time goes in v3:
time: 210 us
  waiting for transfers between devices  85.4 us (41%)
  Pallas kernels  47.7 us (23%)
  starting transfers between devices  38.7 us (18%)
  matrix products  23.6 us (11%)
  other arithmetic  7.14 us (3%)
  local copies, waits for them, and re-layouts  5.32 us (3%)
    ppermute x12, waiting for transfers between devices, across(): return lax.ppermute(values, 'grp', [(0, 1), (1, 0)])  60.6 us
    pallas_call x2, Pallas kernels, spread(): pl.pallas_call(functools.partial(spread_kernel, both_groups), out_shape=t...  47.7 us
    ppermute x16, waiting for transfers between devices, beside(): return lax.ppermute(values, 'dev', [(i, i ^ bit) for i in range(members)])  18.7 us
    ppermute x16, starting transfers between devices, beside(): return lax.ppermute(values, 'dev', [(i, i ^ bit) for i in range(members)])  15.8 us
    ppermute x3, starting transfers between devices, corner(): return lax.ppermute(values, ('grp', 'dev'), pairs)  12.6 us
    ppermute x12, starting transfers between devices, across(): return lax.ppermute(values, 'grp', [(0, 1), (1, 0)])  10.3 us
    dot_general x32, matrix products, dot_t(): lax.dot_general(a, b, (((1,), (1,)), ((), ())), preferred_element_type=jn...  9.68 us
    dot_general x12, matrix products, by_blocks(): lax.dot_general(blocked.reshape(blocks, part, block), weight.reshape(bloc...  9.11 us
  transfers between devices with their start and end apart: 31, of which 17 were waited for; matrix products, arithmetic and copies ran while one was open for 13% of the time, Pallas kernels for 9%

profile of v3, /device:TPU:10, one launch (start us, length us, event | category | flops | bytes accessed | tf_op | source)
XLA Modules:
  0.0 209.6 jit_solution(15161882346393313792)
XLA Ops:
  0.7 2.2 %multiply_reduce_fusion.1 = f32[256]{0:T(256)S(1)} fusion(bf16[256,4096]{1,0:T(8,128)(2,1)} %param.12), kind=kLoop, calls=%fused_computation.2 | loop fusion | flops 3145472 | bytes 2098176 | tf_op jit(solution)/shard_map/reduce_sum | solution.py:321
  8.9 9.3 %collective-permute-done = bf16[128,2048]{1,0:T(8,128)(2,1)} collective-permute-done((bf16[128,2048]{1,0:T(8,128)(2,1)S(1)}, bf16[128,2048]{1,0:T(8,128)(2,1)}, u32[]{:S(2)}, u32[]{:S(2)}) %collective-permute-start) | collective-permute-done | bytes 524320 | tf_op jit(solution)/shard_map/ppermute | solution.py:124
  24.6 3.8 %collective-permute-done.2 = f32[128,384]{1,0:T(8,128)S(1)} collective-permute-done((f32[128,384]{1,0:T(8,128)S(1)}, f32[128,384]{1,0:T(8,128)S(1)}, u32[]{:S(2)}, u32[]{:S(2)}) %collective-permute-start.2) | collective-permute-done | bytes 196640 | tf_op jit(solution)/shard_map/ppermute | solution.py:124
  28.4 3.7 %collective-permute-done.4 = f32[128,384]{1,0:T(8,128)S(1)} collective-permute-done((f32[128,384]{1,0:T(8,128)S(1)}, f32[128,384]{1,0:T(8,128)S(1)}, u32[]{:S(2)}, u32[]{:S(2)}) %collective-permute-start.4) | collective-permute-done | bytes 196640 | tf_op jit(solution)/shard_map/ppermute | solution.py:124
  36.9 19.0 %shard_map.139 = bf16[2,16,128,256]{3,2,1,0:T(8,128)(2,1)S(1)} custom-call(bf16[2,128,256]{2,1,0:T(8,128)(2,1)S(1)} %copy.36.src_ref), custom_call_target="tpu_custom_call" | custom-call | tf_op jit(solution)/shard_map/pallas_call | solution.py:280
  56.7 3.2 %collective-permute-done.6 = bf16[2048,256]{1,0:T(8,128)(2,1)S(1)} collective-permute-done((bf16[2048,256]{1,0:T(8,128)(2,1)S(1)}, bf16[2048,256]{1,0:T(8,128)(2,1)S(1)}, u32[]{:S(2)}, u32[]{:S(2)}) %collective-permute-start.6) | collective-permute-done | bytes 1048608 | tf_op jit(solution)/shard_map/ppermute | solution.py:124
  62.3 28.6 %shard_map.140 = (bf16[2,16,128,256]{3,2,1,0:T(8,128)(2,1)S(1)}, bf16[2,8,128,256]{3,2,1,0:T(8,128)(2,1)S(1)}) custom-call(bf16[2,128,256]{2,1,0:T(8,128)(2,1)S(1)} %pad_maximum_fusion.7.src_ref), custom_call_target="tpu_custom_call" | custom-call | tf_op jit(solution)/shard_map/pallas_call | solution.py:280
  91.8 3.9 %collective-permute-start.7 = (bf16[256,256]{1,0:T(8,128)(2,1)S(1)}, bf16[256,256]{1,0:T(8,128)(2,1)S(1)}, u32[]{:S(2)}, u32[]{:S(2)}) collective-permute-start(bf16[256,256]{1,0:T(8,128)(2,1)S(1)} %pad_maximum_fusion.6), channel_id=1, source_target_pairs={{8,16},{9,17},{10,18},{11,19},{12,20},{13,21},{14,22},{15,23},{16,... | collective-permute-start | bytes 393224 | tf_op jit(solution)/shard_map/ppermute | solution.py:140
  95.8 3.6 %collective-permute-done.8 = f32[2,128,1]{1,0,2:T(2,128)S(1)} collective-permute-done((f32[2,128,1]{1,0,2:T(2,128)S(1)}, f32[2,128,1]{1,0,2:T(2,128)S(1)}, u32[]{:S(2)}, u32[]{:S(2)}) %collective-permute-start.8) | collective-permute-done | bytes 1056 | tf_op jit(solution)/shard_map/ppermute | solution.py:124
  101.9 2.1 collective-permute-start.21
  104.9 2.0 collective-permute-start.10
  106.9 7.7 %collective-permute-done.20 = f32[128,896]{1,0:T(8,128)S(1)} collective-permute-done((f32[128,896]{1,0:T(8,128)S(1)}, f32[128,896]{1,0:T(8,128)S(1)}, u32[]{:S(2)}, u32[]{:S(2)}) %collective-permute-start.20) | collective-permute-done | bytes 458784 | tf_op jit(solution)/shard_map/ppermute | solution.py:124
  115.4 9.0 %collective-permute-done.21 = f32[128,896]{1,0:T(8,128)S(1)} collective-permute-done((f32[128,896]{1,0:T(8,128)S(1)}, f32[128,896]{1,0:T(8,128)S(1)}, u32[]{:S(2)}, u32[]{:S(2)}) %collective-permute-start.21) | collective-permute-done | bytes 458784 | tf_op jit(solution)/shard_map/ppermute | solution.py:124
  127.8 6.5 %collective-permute-done.9 = f32[128,896]{1,0:T(8,128)S(1)} collective-permute-done((f32[128,896]{1,0:T(8,128)S(1)}, f32[128,896]{1,0:T(8,128)S(1)}, u32[]{:S(2)}, u32[]{:S(2)}) %collective-permute-start.9) | collective-permute-done | bytes 458784 | tf_op jit(solution)/shard_map/ppermute | solution.py:124
  135.0 9.1 %collective-permute-done.10 = f32[128,896]{1,0:T(8,128)S(1)} collective-permute-done((f32[128,896]{1,0:T(8,128)S(1)}, f32[128,896]{1,0:T(8,128)S(1)}, u32[]{:S(2)}, u32[]{:S(2)}) %collective-permute-start.10) | collective-permute-done | bytes 458784 | tf_op jit(solution)/shard_map/ppermute | solution.py:124
  148.2 4.7 %collective-permute-done.14 = bf16[128,896]{1,0:T(8,128)(2,1)S(1)} collective-permute-done((bf16[128,896]{1,0:T(8,128)(2,1)S(1)}, bf16[128,896]{1,0:T(8,128)(2,1)S(1)}, u32[]{:S(2)}, u32[]{:S(2)}) %collective-permute-start.14) | collective-permute-done | bytes 229408 | tf_op jit(solution)/shard_map/ppermute | solution.py:124
  159.3 2.2 %collective-permute-start.23 = (f32[2,128,256]{2,1,0:T(8,128)S(1)}, f32[2,128,256]{2,1,0:T(8,128)S(1)}, u32[]{:S(2)}, u32[]{:S(2)}) collective-permute-start(f32[2,128,256]{2,1,0:T(8,128)S(1)} %dynamic-slice_bitcast_fusion.41), channel_id=1, source_target_pairs={{0,4},{1,5},{2,6},{3,7},{4,0},{5,1},{6,2},{7,3},{8,12},{9,13},{10,... | collective-permute-start | bytes 786440 | tf_op jit(solution)/shard_map/ppermute | solution.py:129
  161.6 2.1 collective-permute-start.16
  163.9 4.0 %collective-permute-done.12 = f32[2,128,256]{2,1,0:T(8,128)S(1)} collective-permute-done((f32[2,128,256]{2,1,0:T(8,128)S(1)}, f32[2,128,256]{2,1,0:T(8,128)S(1)}, u32[]{:S(2)}, u32[]{:S(2)}) %collective-permute-start.12) | collective-permute-done | bytes 262176 | tf_op jit(solution)/shard_map/ppermute | solution.py:129
  167.9 2.7 %collective-permute-start.13 = (f32[128,256]{1,0:T(8,128)S(1)}, f32[128,256]{1,0:T(8,128)S(1)}, u32[]{:S(2)}, u32[]{:S(2)}) collective-permute-start(f32[128,256]{1,0:T(8,128)S(1)} %dynamic-slice_bitcast_fusion.47), channel_id=1, source_target_pairs={{0,4},{1,5},{2,6},{3,7},{4,0},{5,1},{6,2},{7,3},{8,12},{9,13},{10,... | collective-permute-start | bytes 393224 | tf_op jit(solution)/shard_map/ppermute | solution.py:129
  170.8 5.7 %collective-permute-done.13 = f32[128,256]{1,0:T(8,128)S(1)} collective-permute-done((f32[128,256]{1,0:T(8,128)S(1)}, f32[128,256]{1,0:T(8,128)S(1)}, u32[]{:S(2)}, u32[]{:S(2)}) %collective-permute-start.13) | collective-permute-done | bytes 131104 | tf_op jit(solution)/shard_map/ppermute | solution.py:129
  185.1 5.8 %collective-permute-done.18 = f32[128,256]{1,0:T(8,128)S(1)} collective-permute-done((f32[128,256]{1,0:T(8,128)S(1)}, f32[128,256]{1,0:T(8,128)S(1)}, u32[]{:S(2)}, u32[]{:S(2)}) %collective-permute-start.18) | collective-permute-done | bytes 131104 | tf_op jit(solution)/shard_map/ppermute | solution.py:129
  192.7 6.7 %collective-permute-start.19 = (bf16[128,256]{1,0:T(8,128)(2,1)S(1)}, bf16[128,256]{1,0:T(8,128)(2,1)S(1)}, u32[]{:S(2)}, u32[]{:S(2)}) collective-permute-start(bf16[128,256]{1,0:T(8,128)(2,1)S(1)} %get-tuple-element.29), channel_id=1, source_target_pairs={{8,16},{9,17},{10,18},{11,19},{12,20},{13,21},{14,22},{15,23},{16,... | collective-permute-start | bytes 196616 | tf_op jit(solution)/shard_map/ppermute | solution.py:140
  203.0 6.0 %collective-permute-done.30 = bf16[128,256]{1,0:T(8,128)(2,1)S(1)} collective-permute-done((bf16[128,256]{1,0:T(8,128)(2,1)S(1)}, bf16[128,256]{1,0:T(8,128)(2,1)S(1)}, u32[]{:S(2)}, u32[]{:S(2)}) %collective-permute-start.30) | collective-permute-done | bytes 65568 | tf_op jit(solution)/shard_map/ppermute | solution.py:140
  (181 shorter events, 54.2 us)
Async XLA Ops:
  2.9 16.0 %collective-permute-start.1 = (f32[256,1]{0,1:T(1,128)S(1)}, f32[256,1]{0,1:T(1,128)S(1)}, u32[]{:S(2)}, u32[]{:S(2)}) collective-permute-start(f32[256,1]{0,1:T(1,128)S(1)} %bitcast.448), channel_id=1, source_target_pairs={{0,16},{16,0},{1,17},{17,1},{2,18},{18,2},{3,19},{19,3},{4,20},{20... | collective-permute-start | bytes 3080 | tf_op jit(solution)/shard_map/ppermute | solution.py:124
  4.6 13.6 %collective-permute-start = (bf16[128,2048]{1,0:T(8,128)(2,1)S(1)}, bf16[128,2048]{1,0:T(8,128)(2,1)}, u32[]{:S(2)}, u32[]{:S(2)}) collective-permute-start(bf16[128,2048]{1,0:T(8,128)(2,1)S(1)} %dynamic_slice.120), channel_id=1, source_target_pairs={{0,16},{16,0},{1,17},{17,1},{2,18},{18,2},{3,19},{19,3},{4,20},{20... | collective-permute-start | bytes 1572872 | tf_op jit(solution)/shard_map/ppermute | solution.py:124
  20.6 7.8 %collective-permute-start.2 = (f32[128,384]{1,0:T(8,128)S(1)}, f32[128,384]{1,0:T(8,128)S(1)}, u32[]{:S(2)}, u32[]{:S(2)}) collective-permute-start(f32[128,384]{1,0:T(8,128)S(1)} %fusion.19), channel_id=1, source_target_pairs={{0,16},{16,0},{1,17},{17,1},{2,18},{18,2},{3,19},{19,3},{4,20},{20... | collective-permute-start | bytes 589832 | tf_op jit(solution)/shard_map/ppermute | solution.py:124
  23.8 8.3 %collective-permute-start.4 = (f32[128,384]{1,0:T(8,128)S(1)}, f32[128,384]{1,0:T(8,128)S(1)}, u32[]{:S(2)}, u32[]{:S(2)}) collective-permute-start(f32[128,384]{1,0:T(8,128)S(1)} %fusion.20), channel_id=1, source_target_pairs={{0,16},{16,0},{1,17},{17,1},{2,18},{18,2},{3,19},{19,3},{4,20},{20... | collective-permute-start | bytes 589832 | tf_op jit(solution)/shard_map/ppermute | solution.py:124
  34.3 25.6 %collective-permute-start.6 = (bf16[2048,256]{1,0:T(8,128)(2,1)S(1)}, bf16[2048,256]{1,0:T(8,128)(2,1)S(1)}, u32[]{:S(2)}, u32[]{:S(2)}) collective-permute-start(bf16[2048,256]{1,0:T(8,128)(2,1)S(1)} %copy-done.3), channel_id=1, source_target_pairs={{0,16},{16,0},{1,17},{17,1},{2,18},{18,2},{3,19},{19,3},{4,20},{20... | collective-permute-start | bytes 3145736 | tf_op jit(solution)/shard_map/ppermute | solution.py:124
  91.8 93.3 %collective-permute-start.7 = (bf16[256,256]{1,0:T(8,128)(2,1)S(1)}, bf16[256,256]{1,0:T(8,128)(2,1)S(1)}, u32[]{:S(2)}, u32[]{:S(2)}) collective-permute-start(bf16[256,256]{1,0:T(8,128)(2,1)S(1)} %pad_maximum_fusion.6), channel_id=1, source_target_pairs={{8,16},{9,17},{10,18},{11,19},{12,20},{13,21},{14,22},{15,23},{16,... | collective-permute-start | bytes 393224 | tf_op jit(solution)/shard_map/ppermute | solution.py:140
  101.1 13.5 %collective-permute-start.20 = (f32[128,896]{1,0:T(8,128)S(1)}, f32[128,896]{1,0:T(8,128)S(1)}, u32[]{:S(2)}, u32[]{:S(2)}) collective-permute-start(f32[128,896]{1,0:T(8,128)S(1)} %convolution_bitcast_fusion.2), channel_id=1, source_target_pairs={{0,16},{16,0},{1,17},{17,1},{2,18},{18,2},{3,19},{19,3},{4,20},{20... | collective-permute-start | bytes 1376264 | tf_op jit(solution)/shard_map/ppermute | solution.py:124
  101.9 22.5 %collective-permute-start.21 = (f32[128,896]{1,0:T(8,128)S(1)}, f32[128,896]{1,0:T(8,128)S(1)}, u32[]{:S(2)}, u32[]{:S(2)}) collective-permute-start(f32[128,896]{1,0:T(8,128)S(1)} %convolution_bitcast_fusion), channel_id=1, source_target_pairs={{0,16},{16,0},{1,17},{17,1},{2,18},{18,2},{3,19},{19,3},{4,20},{20... | collective-permute-start | bytes 1376264 | tf_op jit(solution)/shard_map/ppermute | solution.py:124
  104.8 29.5 %collective-permute-start.9 = (f32[128,896]{1,0:T(8,128)S(1)}, f32[128,896]{1,0:T(8,128)S(1)}, u32[]{:S(2)}, u32[]{:S(2)}) collective-permute-start(f32[128,896]{1,0:T(8,128)S(1)} %convolution_bitcast_fusion.6), channel_id=1, source_target_pairs={{0,16},{16,0},{1,17},{17,1},{2,18},{18,2},{3,19},{19,3},{4,20},{20... | collective-permute-start | bytes 1376264 | tf_op jit(solution)/shard_map/ppermute | solution.py:124
  104.9 39.2 %collective-permute-start.10 = (f32[128,896]{1,0:T(8,128)S(1)}, f32[128,896]{1,0:T(8,128)S(1)}, u32[]{:S(2)}, u32[]{:S(2)}) collective-permute-start(f32[128,896]{1,0:T(8,128)S(1)} %convolution_bitcast_fusion.4), channel_id=1, source_target_pairs={{0,16},{16,0},{1,17},{17,1},{2,18},{18,2},{3,19},{19,3},{4,20},{20... | collective-permute-start | bytes 1376264 | tf_op jit(solution)/shard_map/ppermute | solution.py:124
  126.8 27.4 %collective-permute-start.25 = (bf16[128,896]{1,0:T(8,128)(2,1)S(1)}, bf16[128,896]{1,0:T(8,128)(2,1)S(1)}, u32[]{:S(2)}, u32[]{:S(2)}) collective-permute-start(bf16[128,896]{1,0:T(8,128)(2,1)S(1)} %multiply_convert_fusion.10), channel_id=1, source_target_pairs={{0,16},{16,0},{1,17},{17,1},{2,18},{18,2},{3,19},{19,3},{4,20},{20... | collective-permute-start | bytes 688136 | tf_op jit(solution)/shard_map/ppermute | solution.py:124
  146.9 11.6 %collective-permute-start.11 = (f32[4,128,256]{2,1,0:T(8,128)S(1)}, f32[4,128,256]{2,1,0:T(8,128)S(1)}, u32[]{:S(2)}, u32[]{:S(2)}) collective-permute-start(f32[4,128,256]{2,1,0:T(8,128)S(1)} %pad_maximum_fusion.1), channel_id=1, source_target_pairs={{0,1},{1,0},{2,3},{3,2},{4,5},{5,4},{6,7},{7,6},{8,9},{9,8},{10,11... | collective-permute-start | bytes 1572872 | tf_op jit(solution)/shard_map/ppermute | solution.py:129
  147.0 12.2 %collective-permute-start.22 = (f32[4,128,256]{2,1,0:T(8,128)S(1)}, f32[4,128,256]{2,1,0:T(8,128)S(1)}, u32[]{:S(2)}, u32[]{:S(2)}) collective-permute-start(f32[4,128,256]{2,1,0:T(8,128)S(1)} %pad_maximum_fusion.3), channel_id=1, source_target_pairs={{0,1},{1,0},{2,3},{3,2},{4,5},{5,4},{6,7},{7,6},{8,9},{9,8},{10,11... | collective-permute-start | bytes 1572872 | tf_op jit(solution)/shard_map/ppermute | solution.py:129
  154.1 7.4 %collective-permute-start.15 = (f32[4,128,256]{2,1,0:T(8,128)S(1)}, f32[4,128,256]{2,1,0:T(8,128)S(1)}, u32[]{:S(2)}, u32[]{:S(2)}) collective-permute-start(f32[4,128,256]{2,1,0:T(8,128)S(1)} %pad_maximum_fusion.2), channel_id=1, source_target_pairs={{0,1},{1,0},{2,3},{3,2},{4,5},{5,4},{6,7},{7,6},{8,9},{9,8},{10,11... | collective-permute-start | bytes 1572872 | tf_op jit(solution)/shard_map/ppermute | solution.py:129
  155.5 8.2 %collective-permute-start.26 = (f32[4,128,256]{2,1,0:T(8,128)S(1)}, f32[4,128,256]{2,1,0:T(8,128)S(1)}, u32[]{:S(2)}, u32[]{:S(2)}) collective-permute-start(f32[4,128,256]{2,1,0:T(8,128)S(1)} %pad_maximum_fusion.4), channel_id=1, source_target_pairs={{0,1},{1,0},{2,3},{3,2},{4,5},{5,4},{6,7},{7,6},{8,9},{9,8},{10,11... | collective-permute-start | bytes 1572872 | tf_op jit(solution)/shard_map/ppermute | solution.py:129
  158.6 9.2 %collective-permute-start.12 = (f32[2,128,256]{2,1,0:T(8,128)S(1)}, f32[2,128,256]{2,1,0:T(8,128)S(1)}, u32[]{:S(2)}, u32[]{:S(2)}) collective-permute-start(f32[2,128,256]{2,1,0:T(8,128)S(1)} %dynamic-slice_bitcast_fusion.43), channel_id=1, source_target_pairs={{0,2},{1,3},{2,0},{3,1},{4,6},{5,7},{6,4},{7,5},{8,10},{9,11},{10,... | collective-permute-start | bytes 786440 | tf_op jit(solution)/shard_map/ppermute | solution.py:129
  159.3 11.3 %collective-permute-start.23 = (f32[2,128,256]{2,1,0:T(8,128)S(1)}, f32[2,128,256]{2,1,0:T(8,128)S(1)}, u32[]{:S(2)}, u32[]{:S(2)}) collective-permute-start(f32[2,128,256]{2,1,0:T(8,128)S(1)} %dynamic-slice_bitcast_fusion.41), channel_id=1, source_target_pairs={{0,4},{1,5},{2,6},{3,7},{4,0},{5,1},{6,2},{7,3},{8,12},{9,13},{10,... | collective-permute-start | bytes 786440 | tf_op jit(solution)/shard_map/ppermute | solution.py:129
  161.6 14.9 %collective-permute-start.16 = (f32[2,128,256]{2,1,0:T(8,128)S(1)}, f32[2,128,256]{2,1,0:T(8,128)S(1)}, u32[]{:S(2)}, u32[]{:S(2)}) collective-permute-start(f32[2,128,256]{2,1,0:T(8,128)S(1)} %dynamic-slice_bitcast_fusion.42), channel_id=1, source_target_pairs={{0,2},{1,3},{2,0},{3,1},{4,6},{5,7},{6,4},{7,5},{8,10},{9,11},{10,... | collective-permute-start | bytes 786440 | tf_op jit(solution)/shard_map/ppermute | solution.py:129
  163.8 14.6 %collective-permute-start.27 = (f32[2,128,256]{2,1,0:T(8,128)S(1)}, f32[2,128,256]{2,1,0:T(8,128)S(1)}, u32[]{:S(2)}, u32[]{:S(2)}) collective-permute-start(f32[2,128,256]{2,1,0:T(8,128)S(1)} %dynamic-slice_bitcast_fusion.40), channel_id=1, source_target_pairs={{0,4},{1,5},{2,6},{3,7},{4,0},{5,1},{6,2},{7,3},{8,12},{9,13},{10,... | collective-permute-start | bytes 786440 | tf_op jit(solution)/shard_map/ppermute | solution.py:129
  167.9 8.5 %collective-permute-start.13 = (f32[128,256]{1,0:T(8,128)S(1)}, f32[128,256]{1,0:T(8,128)S(1)}, u32[]{:S(2)}, u32[]{:S(2)}) collective-permute-start(f32[128,256]{1,0:T(8,128)S(1)} %dynamic-slice_bitcast_fusion.47), channel_id=1, source_target_pairs={{0,4},{1,5},{2,6},{3,7},{4,0},{5,1},{6,2},{7,3},{8,12},{9,13},{10,... | collective-permute-start | bytes 393224 | tf_op jit(solution)/shard_map/ppermute | solution.py:129
  181.7 9.3 %collective-permute-start.18 = (f32[128,256]{1,0:T(8,128)S(1)}, f32[128,256]{1,0:T(8,128)S(1)}, u32[]{:S(2)}, u32[]{:S(2)}) collective-permute-start(f32[128,256]{1,0:T(8,128)S(1)} %fusion.48), channel_id=1, source_target_pairs={{0,8},{1,9},{2,10},{3,11},{4,12},{5,13},{6,14},{7,15},{8,0},{9,1},... | collective-permute-start | bytes 393224 | tf_op jit(solution)/shard_map/ppermute | solution.py:129
  183.5 9.1 %collective-permute-start.29 = (f32[128,256]{1,0:T(8,128)S(1)}, f32[128,256]{1,0:T(8,128)S(1)}, u32[]{:S(2)}, u32[]{:S(2)}) collective-permute-start(f32[128,256]{1,0:T(8,128)S(1)} %fusion.41), channel_id=1, source_target_pairs={{0,8},{1,9},{2,10},{3,11},{4,12},{5,13},{6,14},{7,15},{8,0},{9,1},... | collective-permute-start | bytes 393224 | tf_op jit(solution)/shard_map/ppermute | solution.py:129
  192.7 10.2 %collective-permute-start.19 = (bf16[128,256]{1,0:T(8,128)(2,1)S(1)}, bf16[128,256]{1,0:T(8,128)(2,1)S(1)}, u32[]{:S(2)}, u32[]{:S(2)}) collective-permute-start(bf16[128,256]{1,0:T(8,128)(2,1)S(1)} %get-tuple-element.29), channel_id=1, source_target_pairs={{8,16},{9,17},{10,18},{11,19},{12,20},{13,21},{14,22},{15,23},{16,... | collective-permute-start | bytes 196616 | tf_op jit(solution)/shard_map/ppermute | solution.py:140
  201.0 7.9 %collective-permute-start.30 = (bf16[128,256]{1,0:T(8,128)(2,1)S(1)}, bf16[128,256]{1,0:T(8,128)(2,1)S(1)}, u32[]{:S(2)}, u32[]{:S(2)}) collective-permute-start(bf16[128,256]{1,0:T(8,128)(2,1)S(1)} %get-tuple-element.30), channel_id=1, source_target_pairs={{8,16},{9,17},{10,18},{11,19},{12,20},{13,21},{14,22},{15,23},{16,... | collective-permute-start | bytes 196616 | tf_op jit(solution)/shard_map/ppermute | solution.py:140
  (16 other events, 172.6 us)

commit v4 on v3

--- a/solution.py
+++ b/solution.py
@@ -15,7 +15,7 @@
 
 
 rope_base = 500000.0
-wire = jnp.float32
+wire = jnp.bfloat16
 
 
 def norm_rows(values, gain):

time: 210 us -> 181 us (0.86)
  waiting for transfers between devices: 85.4 us -> 58.3 us
  starting transfers between devices: 38.7 us -> 36.2 us
    ppermute x12, waiting for transfers between devices: 60.6 us -> 38.5 us  [across(): return lax.ppermute(values, 'grp', [(0, 1), (1, 0)])]
    ppermute x16, waiting for transfers between devices: 18.7 us -> 16.2 us  [beside(): return lax.ppermute(values, 'dev', [(i, i ^ bit) for i in range(members)])]
    ppermute x3, waiting for transfers between devices: 6 us -> 3.62 us  [corner(): return lax.ppermute(values, ('grp', 'dev'), pairs)]
  transfers between devices with their start and end apart: 31 -> 31, of which waited for: 17 -> 21; matrix products, arithmetic and copies ran while one was open for 13% -> 15% of each run, Pallas kernels for 9% -> 11%
where the time goes in v4:
time: 181 us; the launch traced here: 180 us
  waiting for transfers between devices  58.3 us (32%)
  Pallas kernels  46.7 us (26%)
  starting transfers between devices  36.2 us (20%)
  matrix products  23.6 us (13%)
  other arithmetic  7.32 us (4%)
  local copies, waits for them, and re-layouts  6.41 us (4%)
  between operations  1.85 us (1%)
    pallas_call x2, Pallas kernels, spread(): pl.pallas_call(functools.partial(spread_kernel, both_groups), out_shape=t...  46.7 us
    ppermute x12, waiting for transfers between devices, across(): return lax.ppermute(values, 'grp', [(0, 1), (1, 0)])  38.5 us
    ppermute x16, waiting for transfers between devices, beside(): return lax.ppermute(values, 'dev', [(i, i ^ bit) for i in range(members)])  16.2 us
    ppermute x16, starting transfers between devices, beside(): return lax.ppermute(values, 'dev', [(i, i ^ bit) for i in range(members)])  14.1 us
    ppermute x3, starting transfers between devices, corner(): return lax.ppermute(values, ('grp', 'dev'), pairs)  11.3 us
    ppermute x12, starting transfers between devices, across(): return lax.ppermute(values, 'grp', [(0, 1), (1, 0)])  10.8 us
    dot_general x32, matrix products, dot_t(): lax.dot_general(a, b, (((1,), (1,)), ((), ())), preferred_element_type=jn...  9.7 us
    dot_general x12, matrix products, by_blocks(): lax.dot_general(blocked.reshape(blocks, part, block), weight.reshape(bloc...  9.06 us
  transfers between devices with their start and end apart: 31, of which 21 were waited for; matrix products, arithmetic and copies ran while one was open for 15% of the time, Pallas kernels for 11%

profile of v4, /device:TPU:10, one launch (start us, length us, event | category | flops | bytes accessed | tf_op | source)
XLA Modules:
  0.0 180.4 jit_solution(5879938235501742911)
XLA Ops:
  2.5 2.1 %multiply_reduce_fusion.1 = f32[256]{0:T(256)S(1)} fusion(bf16[256,4096]{1,0:T(8,128)(2,1)} %param.12), kind=kLoop, calls=%fused_computation.2 | loop fusion | flops 3145472 | bytes 2098176 | tf_op jit(solution)/shard_map/reduce_sum | solution.py:321
  8.9 6.9 %collective-permute-done = bf16[128,2048]{1,0:T(8,128)(2,1)} collective-permute-done((bf16[128,2048]{1,0:T(8,128)(2,1)S(1)}, bf16[128,2048]{1,0:T(8,128)(2,1)}, u32[]{:S(2)}, u32[]{:S(2)}) %collective-permute-start) | collective-permute-done | bytes 524320 | tf_op jit(solution)/shard_map/ppermute | solution.py:124
  22.2 3.9 %collective-permute-done.2 = f32[128,384]{1,0:T(8,128)S(1)} collective-permute-done((f32[128,384]{1,0:T(8,128)S(1)}, f32[128,384]{1,0:T(8,128)S(1)}, u32[]{:S(2)}, u32[]{:S(2)}) %collective-permute-start.2) | collective-permute-done | bytes 196640 | tf_op jit(solution)/shard_map/ppermute | solution.py:124
  26.0 3.7 %collective-permute-done.4 = f32[128,384]{1,0:T(8,128)S(1)} collective-permute-done((f32[128,384]{1,0:T(8,128)S(1)}, f32[128,384]{1,0:T(8,128)S(1)}, u32[]{:S(2)}, u32[]{:S(2)}) %collective-permute-start.4) | collective-permute-done | bytes 196640 | tf_op jit(solution)/shard_map/ppermute | solution.py:124
  33.8 19.0 %shard_map.139 = bf16[2,16,128,256]{3,2,1,0:T(8,128)(2,1)S(1)} custom-call(bf16[2,128,256]{2,1,0:T(8,128)(2,1)S(1)} %copy.48.src_ref), custom_call_target="tpu_custom_call" | custom-call | tf_op jit(solution)/shard_map/pallas_call | solution.py:280
  53.6 3.9 %collective-permute-done.6 = bf16[2048,256]{1,0:T(8,128)(2,1)S(1)} collective-permute-done((bf16[2048,256]{1,0:T(8,128)(2,1)S(1)}, bf16[2048,256]{1,0:T(8,128)(2,1)S(1)}, u32[]{:S(2)}, u32[]{:S(2)}) %collective-permute-start.6) | collective-permute-done | bytes 1048608 | tf_op jit(solution)/shard_map/ppermute | solution.py:124
  59.9 27.7 %shard_map.140 = (bf16[2,16,128,256]{3,2,1,0:T(8,128)(2,1)S(1)}, bf16[2,8,128,256]{3,2,1,0:T(8,128)(2,1)S(1)}) custom-call(bf16[2,128,256]{2,1,0:T(8,128)(2,1)S(1)} %pad_maximum_fusion.7.src_ref), custom_call_target="tpu_custom_call" | custom-call | tf_op jit(solution)/shard_map/pallas_call | solution.py:280
  94.1 3.7 %collective-permute-start.7 = (bf16[256,256]{1,0:T(8,128)(2,1)S(1)}, bf16[256,256]{1,0:T(8,128)(2,1)S(1)}, u32[]{:S(2)}, u32[]{:S(2)}) collective-permute-start(bf16[256,256]{1,0:T(8,128)(2,1)S(1)} %pad_maximum_fusion.6), channel_id=1, source_target_pairs={{8,16},{9,17},{10,18},{11,19},{12,20},{13,21},{14,22},{15,23},{16,... | collective-permute-start | bytes 393224 | tf_op jit(solution)/shard_map/ppermute | solution.py:140
  99.4 2.0 %collective-permute-start.9 = (bf16[128,896]{1,0:T(8,128)(2,1)S(1)}, bf16[128,896]{1,0:T(8,128)(2,1)S(1)}, u32[]{:S(2)}, u32[]{:S(2)}) collective-permute-start(bf16[128,896]{1,0:T(8,128)(2,1)S(1)} %fusion.2), channel_id=1, source_target_pairs={{0,16},{16,0},{1,17},{17,1},{2,18},{18,2},{3,19},{19,3},{4,20},{20... | collective-permute-start | bytes 688136 | tf_op jit(solution)/shard_map/ppermute | solution.py:124
  103.2 2.0 %collective-permute-start.20 = (bf16[128,896]{1,0:T(8,128)(2,1)S(1)}, bf16[128,896]{1,0:T(8,128)(2,1)S(1)}, u32[]{:S(2)}, u32[]{:S(2)}) collective-permute-start(bf16[128,896]{1,0:T(8,128)(2,1)S(1)} %fusion.4), channel_id=1, source_target_pairs={{0,16},{16,0},{1,17},{17,1},{2,18},{18,2},{3,19},{19,3},{4,20},{20... | collective-permute-start | bytes 688136 | tf_op jit(solution)/shard_map/ppermute | solution.py:124
  105.2 3.2 %collective-permute-done.10 = bf16[128,896]{1,0:T(8,128)(2,1)S(1)} collective-permute-done((bf16[128,896]{1,0:T(8,128)(2,1)S(1)}, bf16[128,896]{1,0:T(8,128)(2,1)S(1)}, u32[]{:S(2)}, u32[]{:S(2)}) %collective-permute-start.10) | collective-permute-done | bytes 229408 | tf_op jit(solution)/shard_map/ppermute | solution.py:124
  108.4 4.9 %collective-permute-done.9 = bf16[128,896]{1,0:T(8,128)(2,1)S(1)} collective-permute-done((bf16[128,896]{1,0:T(8,128)(2,1)S(1)}, bf16[128,896]{1,0:T(8,128)(2,1)S(1)}, u32[]{:S(2)}, u32[]{:S(2)}) %collective-permute-start.9) | collective-permute-done | bytes 229408 | tf_op jit(solution)/shard_map/ppermute | solution.py:124
  116.1 2.2 %collective-permute-done.21 = bf16[128,896]{1,0:T(8,128)(2,1)S(1)} collective-permute-done((bf16[128,896]{1,0:T(8,128)(2,1)S(1)}, bf16[128,896]{1,0:T(8,128)(2,1)S(1)}, u32[]{:S(2)}, u32[]{:S(2)}) %collective-permute-start.21) | collective-permute-done | bytes 229408 | tf_op jit(solution)/shard_map/ppermute | solution.py:124
  118.2 4.9 %collective-permute-done.20 = bf16[128,896]{1,0:T(8,128)(2,1)S(1)} collective-permute-done((bf16[128,896]{1,0:T(8,128)(2,1)S(1)}, bf16[128,896]{1,0:T(8,128)(2,1)S(1)}, u32[]{:S(2)}, u32[]{:S(2)}) %collective-permute-start.20) | collective-permute-done | bytes 229408 | tf_op jit(solution)/shard_map/ppermute | solution.py:124
  129.4 3.4 %collective-permute-done.25 = bf16[128,896]{1,0:T(8,128)(2,1)S(1)} collective-permute-done((bf16[128,896]{1,0:T(8,128)(2,1)S(1)}, bf16[128,896]{1,0:T(8,128)(2,1)S(1)}, u32[]{:S(2)}, u32[]{:S(2)}) %collective-permute-start.25) | collective-permute-done | bytes 229408 | tf_op jit(solution)/shard_map/ppermute | solution.py:124
  137.3 3.6 %collective-permute-start.23 = (bf16[2,128,256]{2,1,0:T(8,128)(2,1)S(1)}, bf16[2,128,256]{2,1,0:T(8,128)(2,1)S(1)}, u32[]{:S(2)}, u32[]{:S(2)}) collective-permute-start(bf16[2,128,256]{2,1,0:T(8,128)(2,1)S(1)} %fusion.40), channel_id=1, source_target_pairs={{0,4},{1,5},{2,6},{3,7},{4,0},{5,1},{6,2},{7,3},{8,12},{9,13},{10,... | collective-permute-start | bytes 393224 | tf_op jit(solution)/shard_map/ppermute | solution.py:129
  140.8 2.0 %collective-permute-done.12 = bf16[2,128,256]{2,1,0:T(8,128)(2,1)S(1)} collective-permute-done((bf16[2,128,256]{2,1,0:T(8,128)(2,1)S(1)}, bf16[2,128,256]{2,1,0:T(8,128)(2,1)S(1)}, u32[]{:S(2)}, u32[]{:S(2)}) %collective-permute-start.12) | collective-permute-done | bytes 131104 | tf_op jit(solution)/shard_map/ppermute | solution.py:129
  142.8 2.8 %collective-permute-start.13 = (bf16[128,256]{1,0:T(8,128)(2,1)S(1)}, bf16[128,256]{1,0:T(8,128)(2,1)S(1)}, u32[]{:S(2)}, u32[]{:S(2)}) collective-permute-start(bf16[128,256]{1,0:T(8,128)(2,1)S(1)} %fusion.76), channel_id=1, source_target_pairs={{0,4},{1,5},{2,6},{3,7},{4,0},{5,1},{6,2},{7,3},{8,12},{9,13},{10,... | collective-permute-start | bytes 196616 | tf_op jit(solution)/shard_map/ppermute | solution.py:129
  147.9 2.1 %collective-permute-done.24 = bf16[128,256]{1,0:T(8,128)(2,1)S(1)} collective-permute-done((bf16[128,256]{1,0:T(8,128)(2,1)S(1)}, bf16[128,256]{1,0:T(8,128)(2,1)S(1)}, u32[]{:S(2)}, u32[]{:S(2)}) %collective-permute-start.24) | collective-permute-done | bytes 65568 | tf_op jit(solution)/shard_map/ppermute | solution.py:129
  152.2 3.0 %collective-permute-done.16 = bf16[2,128,256]{2,1,0:T(8,128)(2,1)S(1)} collective-permute-done((bf16[2,128,256]{2,1,0:T(8,128)(2,1)S(1)}, bf16[2,128,256]{2,1,0:T(8,128)(2,1)S(1)}, u32[]{:S(2)}, u32[]{:S(2)}) %collective-permute-start.16) | collective-permute-done | bytes 131104 | tf_op jit(solution)/shard_map/ppermute | solution.py:129
  163.2 2.1 %collective-permute-done.18 = bf16[128,256]{1,0:T(8,128)(2,1)S(1)} collective-permute-done((bf16[128,256]{1,0:T(8,128)(2,1)S(1)}, bf16[128,256]{1,0:T(8,128)(2,1)S(1)}, u32[]{:S(2)}, u32[]{:S(2)}) %collective-permute-start.18) | collective-permute-done | bytes 65568 | tf_op jit(solution)/shard_map/ppermute | solution.py:129
  166.9 3.3 %collective-permute-start.30 = (bf16[128,256]{1,0:T(8,128)(2,1)S(1)}, bf16[128,256]{1,0:T(8,128)(2,1)S(1)}, u32[]{:S(2)}, u32[]{:S(2)}) collective-permute-start(bf16[128,256]{1,0:T(8,128)(2,1)S(1)} %get-tuple-element.33), channel_id=1, source_target_pairs={{8,16},{9,17},{10,18},{11,19},{12,20},{13,21},{14,22},{15,23},{16,... | collective-permute-start | bytes 196616 | tf_op jit(solution)/shard_map/ppermute | solution.py:140
  171.7 4.3 %collective-permute-start.19 = (bf16[128,256]{1,0:T(8,128)(2,1)S(1)}, bf16[128,256]{1,0:T(8,128)(2,1)S(1)}, u32[]{:S(2)}, u32[]{:S(2)}) collective-permute-start(bf16[128,256]{1,0:T(8,128)(2,1)S(1)} %get-tuple-element.32), channel_id=1, source_target_pairs={{8,16},{9,17},{10,18},{11,19},{12,20},{13,21},{14,22},{15,23},{16,... | collective-permute-start | bytes 196616 | tf_op jit(solution)/shard_map/ppermute | solution.py:140
  176.1 3.6 %collective-permute-done.19 = bf16[128,256]{1,0:T(8,128)(2,1)S(1)} collective-permute-done((bf16[128,256]{1,0:T(8,128)(2,1)S(1)}, bf16[128,256]{1,0:T(8,128)(2,1)S(1)}, u32[]{:S(2)}, u32[]{:S(2)}) %collective-permute-start.19) | collective-permute-done | bytes 65568 | tf_op jit(solution)/shard_map/ppermute | solution.py:140
  (183 shorter events, 58.3 us)
Async XLA Ops:
  1.9 13.8 %collective-permute-start = (bf16[128,2048]{1,0:T(8,128)(2,1)S(1)}, bf16[128,2048]{1,0:T(8,128)(2,1)}, u32[]{:S(2)}, u32[]{:S(2)}) collective-permute-start(bf16[128,2048]{1,0:T(8,128)(2,1)S(1)} %dynamic_slice.120), channel_id=1, source_target_pairs={{0,16},{16,0},{1,17},{17,1},{2,18},{18,2},{3,19},{19,3},{4,20},{20... | collective-permute-start | bytes 1572872 | tf_op jit(solution)/shard_map/ppermute | solution.py:124
  4.6 12.0 %collective-permute-start.1 = (f32[256,1]{0,1:T(1,128)S(1)}, f32[256,1]{0,1:T(1,128)S(1)}, u32[]{:S(2)}, u32[]{:S(2)}) collective-permute-start(f32[256,1]{0,1:T(1,128)S(1)} %bitcast.448), channel_id=1, source_target_pairs={{0,16},{16,0},{1,17},{17,1},{2,18},{18,2},{3,19},{19,3},{4,20},{20... | collective-permute-start | bytes 3080 | tf_op jit(solution)/shard_map/ppermute | solution.py:124
  18.3 7.8 %collective-permute-start.2 = (f32[128,384]{1,0:T(8,128)S(1)}, f32[128,384]{1,0:T(8,128)S(1)}, u32[]{:S(2)}, u32[]{:S(2)}) collective-permute-start(f32[128,384]{1,0:T(8,128)S(1)} %fusion.19), channel_id=1, source_target_pairs={{0,16},{16,0},{1,17},{17,1},{2,18},{18,2},{3,19},{19,3},{4,20},{20... | collective-permute-start | bytes 589832 | tf_op jit(solution)/shard_map/ppermute | solution.py:124
  20.5 9.2 %collective-permute-start.4 = (f32[128,384]{1,0:T(8,128)S(1)}, f32[128,384]{1,0:T(8,128)S(1)}, u32[]{:S(2)}, u32[]{:S(2)}) collective-permute-start(f32[128,384]{1,0:T(8,128)S(1)} %fusion.20), channel_id=1, source_target_pairs={{0,16},{16,0},{1,17},{17,1},{2,18},{18,2},{3,19},{19,3},{4,20},{20... | collective-permute-start | bytes 589832 | tf_op jit(solution)/shard_map/ppermute | solution.py:124
  31.9 25.6 %collective-permute-start.6 = (bf16[2048,256]{1,0:T(8,128)(2,1)S(1)}, bf16[2048,256]{1,0:T(8,128)(2,1)S(1)}, u32[]{:S(2)}, u32[]{:S(2)}) collective-permute-start(bf16[2048,256]{1,0:T(8,128)(2,1)S(1)} %copy-done.3), channel_id=1, source_target_pairs={{0,16},{16,0},{1,17},{17,1},{2,18},{18,2},{3,19},{19,3},{4,20},{20... | collective-permute-start | bytes 3145736 | tf_op jit(solution)/shard_map/ppermute | solution.py:124
  92.5 5.2 %collective-permute-start.8 = (f32[2,128,1]{1,0,2:T(2,128)S(1)}, f32[2,128,1]{1,0,2:T(2,128)S(1)}, u32[]{:S(2)}, u32[]{:S(2)}) collective-permute-start(f32[2,128,1]{1,0,2:T(2,128)S(1)} %get-tuple-element.42), channel_id=1, source_target_pairs={{0,16},{16,0},{1,17},{17,1},{2,18},{18,2},{3,19},{19,3},{4,20},{20... | collective-permute-start | bytes 3080 | tf_op jit(solution)/shard_map/ppermute | solution.py:124
  94.1 69.1 %collective-permute-start.7 = (bf16[256,256]{1,0:T(8,128)(2,1)S(1)}, bf16[256,256]{1,0:T(8,128)(2,1)S(1)}, u32[]{:S(2)}, u32[]{:S(2)}) collective-permute-start(bf16[256,256]{1,0:T(8,128)(2,1)S(1)} %pad_maximum_fusion.6), channel_id=1, source_target_pairs={{8,16},{9,17},{10,18},{11,19},{12,20},{13,21},{14,22},{15,23},{16,... | collective-permute-start | bytes 393224 | tf_op jit(solution)/shard_map/ppermute | solution.py:140
  99.4 9.0 %collective-permute-start.10 = (bf16[128,896]{1,0:T(8,128)(2,1)S(1)}, bf16[128,896]{1,0:T(8,128)(2,1)S(1)}, u32[]{:S(2)}, u32[]{:S(2)}) collective-permute-start(bf16[128,896]{1,0:T(8,128)(2,1)S(1)} %fusion.3), channel_id=1, source_target_pairs={{0,16},{16,0},{1,17},{17,1},{2,18},{18,2},{3,19},{19,3},{4,20},{20... | collective-permute-start | bytes 688136 | tf_op jit(solution)/shard_map/ppermute | solution.py:124
  99.4 13.9 %collective-permute-start.9 = (bf16[128,896]{1,0:T(8,128)(2,1)S(1)}, bf16[128,896]{1,0:T(8,128)(2,1)S(1)}, u32[]{:S(2)}, u32[]{:S(2)}) collective-permute-start(bf16[128,896]{1,0:T(8,128)(2,1)S(1)} %fusion.2), channel_id=1, source_target_pairs={{0,16},{16,0},{1,17},{17,1},{2,18},{18,2},{3,19},{19,3},{4,20},{20... | collective-permute-start | bytes 688136 | tf_op jit(solution)/shard_map/ppermute | solution.py:124
  102.2 16.0 %collective-permute-start.21 = (bf16[128,896]{1,0:T(8,128)(2,1)S(1)}, bf16[128,896]{1,0:T(8,128)(2,1)S(1)}, u32[]{:S(2)}, u32[]{:S(2)}) collective-permute-start(bf16[128,896]{1,0:T(8,128)(2,1)S(1)} %fusion.5), channel_id=1, source_target_pairs={{0,16},{16,0},{1,17},{17,1},{2,18},{18,2},{3,19},{19,3},{4,20},{20... | collective-permute-start | bytes 688136 | tf_op jit(solution)/shard_map/ppermute | solution.py:124
  103.2 20.0 %collective-permute-start.20 = (bf16[128,896]{1,0:T(8,128)(2,1)S(1)}, bf16[128,896]{1,0:T(8,128)(2,1)S(1)}, u32[]{:S(2)}, u32[]{:S(2)}) collective-permute-start(bf16[128,896]{1,0:T(8,128)(2,1)S(1)} %fusion.4), channel_id=1, source_target_pairs={{0,16},{16,0},{1,17},{17,1},{2,18},{18,2},{3,19},{19,3},{4,20},{20... | collective-permute-start | bytes 688136 | tf_op jit(solution)/shard_map/ppermute | solution.py:124
  115.0 13.0 %collective-permute-start.14 = (bf16[128,896]{1,0:T(8,128)(2,1)S(1)}, bf16[128,896]{1,0:T(8,128)(2,1)S(1)}, u32[]{:S(2)}, u32[]{:S(2)}) collective-permute-start(bf16[128,896]{1,0:T(8,128)(2,1)S(1)} %multiply_convert_fusion.11), channel_id=1, source_target_pairs={{0,16},{16,0},{1,17},{17,1},{2,18},{18,2},{3,19},{19,3},{4,20},{20... | collective-permute-start | bytes 688136 | tf_op jit(solution)/shard_map/ppermute | solution.py:124
  123.3 9.6 %collective-permute-start.25 = (bf16[128,896]{1,0:T(8,128)(2,1)S(1)}, bf16[128,896]{1,0:T(8,128)(2,1)S(1)}, u32[]{:S(2)}, u32[]{:S(2)}) collective-permute-start(bf16[128,896]{1,0:T(8,128)(2,1)S(1)} %multiply_convert_fusion.10), channel_id=1, source_target_pairs={{0,16},{16,0},{1,17},{17,1},{2,18},{18,2},{3,19},{19,3},{4,20},{20... | collective-permute-start | bytes 688136 | tf_op jit(solution)/shard_map/ppermute | solution.py:124
  125.3 11.4 %collective-permute-start.11 = (f32[4,128,256]{2,1,0:T(8,128)S(1)}, f32[4,128,256]{2,1,0:T(8,128)S(1)}, u32[]{:S(2)}, u32[]{:S(2)}) collective-permute-start(f32[4,128,256]{2,1,0:T(8,128)S(1)} %pad_maximum_fusion.1), channel_id=1, source_target_pairs={{0,1},{1,0},{2,3},{3,2},{4,5},{5,4},{6,7},{7,6},{8,9},{9,8},{10,11... | collective-permute-start | bytes 1572872 | tf_op jit(solution)/shard_map/ppermute | solution.py:129
  125.4 11.7 %collective-permute-start.22 = (f32[4,128,256]{2,1,0:T(8,128)S(1)}, f32[4,128,256]{2,1,0:T(8,128)S(1)}, u32[]{:S(2)}, u32[]{:S(2)}) collective-permute-start(f32[4,128,256]{2,1,0:T(8,128)S(1)} %pad_maximum_fusion.3), channel_id=1, source_target_pairs={{0,1},{1,0},{2,3},{3,2},{4,5},{5,4},{6,7},{7,6},{8,9},{9,8},{10,11... | collective-permute-start | bytes 1572872 | tf_op jit(solution)/shard_map/ppermute | solution.py:129
  129.3 20.7 %collective-permute-start.15 = (f32[4,128,256]{2,1,0:T(8,128)S(1)}, f32[4,128,256]{2,1,0:T(8,128)S(1)}, u32[]{:S(2)}, u32[]{:S(2)}) collective-permute-start(f32[4,128,256]{2,1,0:T(8,128)S(1)} %pad_maximum_fusion.2), channel_id=1, source_target_pairs={{0,1},{1,0},{2,3},{3,2},{4,5},{5,4},{6,7},{7,6},{8,9},{9,8},{10,11... | collective-permute-start | bytes 1572872 | tf_op jit(solution)/shard_map/ppermute | solution.py:129
  134.1 17.1 %collective-permute-start.26 = (f32[4,128,256]{2,1,0:T(8,128)S(1)}, f32[4,128,256]{2,1,0:T(8,128)S(1)}, u32[]{:S(2)}, u32[]{:S(2)}) collective-permute-start(f32[4,128,256]{2,1,0:T(8,128)S(1)} %pad_maximum_fusion.4), channel_id=1, source_target_pairs={{0,1},{1,0},{2,3},{3,2},{4,5},{5,4},{6,7},{7,6},{8,9},{9,8},{10,11... | collective-permute-start | bytes 1572872 | tf_op jit(solution)/shard_map/ppermute | solution.py:129
  136.8 6.0 %collective-permute-start.12 = (bf16[2,128,256]{2,1,0:T(8,128)(2,1)S(1)}, bf16[2,128,256]{2,1,0:T(8,128)(2,1)S(1)}, u32[]{:S(2)}, u32[]{:S(2)}) collective-permute-start(bf16[2,128,256]{2,1,0:T(8,128)(2,1)S(1)} %fusion.42), channel_id=1, source_target_pairs={{0,2},{1,3},{2,0},{3,1},{4,6},{5,7},{6,4},{7,5},{8,10},{9,11},{10,... | collective-permute-start | bytes 393224 | tf_op jit(solution)/shard_map/ppermute | solution.py:129
  137.3 8.4 %collective-permute-start.23 = (bf16[2,128,256]{2,1,0:T(8,128)(2,1)S(1)}, bf16[2,128,256]{2,1,0:T(8,128)(2,1)S(1)}, u32[]{:S(2)}, u32[]{:S(2)}) collective-permute-start(bf16[2,128,256]{2,1,0:T(8,128)(2,1)S(1)} %fusion.40), channel_id=1, source_target_pairs={{0,4},{1,5},{2,6},{3,7},{4,0},{5,1},{6,2},{7,3},{8,12},{9,13},{10,... | collective-permute-start | bytes 393224 | tf_op jit(solution)/shard_map/ppermute | solution.py:129
  151.4 5.7 %collective-permute-start.27 = (bf16[2,128,256]{2,1,0:T(8,128)(2,1)S(1)}, bf16[2,128,256]{2,1,0:T(8,128)(2,1)S(1)}, u32[]{:S(2)}, u32[]{:S(2)}) collective-permute-start(bf16[2,128,256]{2,1,0:T(8,128)(2,1)S(1)} %fusion.41), channel_id=1, source_target_pairs={{0,4},{1,5},{2,6},{3,7},{4,0},{5,1},{6,2},{7,3},{8,12},{9,13},{10,... | collective-permute-start | bytes 393224 | tf_op jit(solution)/shard_map/ppermute | solution.py:129
  160.1 5.2 %collective-permute-start.18 = (bf16[128,256]{1,0:T(8,128)(2,1)S(1)}, bf16[128,256]{1,0:T(8,128)(2,1)S(1)}, u32[]{:S(2)}, u32[]{:S(2)}) collective-permute-start(bf16[128,256]{1,0:T(8,128)(2,1)S(1)} %fusion.80), channel_id=1, source_target_pairs={{0,8},{1,9},{2,10},{3,11},{4,12},{5,13},{6,14},{7,15},{8,0},{9,1},... | collective-permute-start | bytes 196616 | tf_op jit(solution)/shard_map/ppermute | solution.py:129
  161.6 5.2 %collective-permute-start.29 = (bf16[128,256]{1,0:T(8,128)(2,1)S(1)}, bf16[128,256]{1,0:T(8,128)(2,1)S(1)}, u32[]{:S(2)}, u32[]{:S(2)}) collective-permute-start(bf16[128,256]{1,0:T(8,128)(2,1)S(1)} %fusion.81), channel_id=1, source_target_pairs={{0,8},{1,9},{2,10},{3,11},{4,12},{5,13},{6,14},{7,15},{8,0},{9,1},... | collective-permute-start | bytes 196616 | tf_op jit(solution)/shard_map/ppermute | solution.py:129
  166.9 9.2 %collective-permute-start.30 = (bf16[128,256]{1,0:T(8,128)(2,1)S(1)}, bf16[128,256]{1,0:T(8,128)(2,1)S(1)}, u32[]{:S(2)}, u32[]{:S(2)}) collective-permute-start(bf16[128,256]{1,0:T(8,128)(2,1)S(1)} %get-tuple-element.33), channel_id=1, source_target_pairs={{8,16},{9,17},{10,18},{11,19},{12,20},{13,21},{14,22},{15,23},{16,... | collective-permute-start | bytes 196616 | tf_op jit(solution)/shard_map/ppermute | solution.py:140
  171.7 7.9 %collective-permute-start.19 = (bf16[128,256]{1,0:T(8,128)(2,1)S(1)}, bf16[128,256]{1,0:T(8,128)(2,1)S(1)}, u32[]{:S(2)}, u32[]{:S(2)}) collective-permute-start(bf16[128,256]{1,0:T(8,128)(2,1)S(1)} %get-tuple-element.32), channel_id=1, source_target_pairs={{8,16},{9,17},{10,18},{11,19},{12,20},{13,21},{14,22},{15,23},{16,... | collective-permute-start | bytes 196616 | tf_op jit(solution)/shard_map/ppermute | solution.py:140
  (16 other events, 145.2 us)
